TPU v7x, 128 devices: a whole 4x4x4 slice. The times are simulated.
128 devices in a mesh: row: 16 (over x, y), col: 8 (over z, core).
Axes of the slice: x: 4, y: 4, z: 4, core: 2. Of those that a mesh axis runs over, the one named last changes fastest.
Arguments:
- pair_rep: bfloat16 [512, 512, 128], P(('row', 'col')), may hold values from -16 to 16
- tile_mask: int32 [4, 4], replicated, may hold values from 0 to 1, as said below
- chain_ids: int32 [512], replicated, may hold values from 0 to 3, never falling along the last dimension, each value on 1 to 256 neighbouring positions
- chain_bias: float32 [2, 4], replicated, may hold values from -6 to 6
- row_project: bfloat16 [128, 512], replicated, may hold values from -0.5 to 0.5
- row_bias_proj: bfloat16 [128, 4], replicated, may hold values from -36 to 36
- row_output: bfloat16 [128, 128], replicated, may hold values from -0.5 to 0.5
- col_project: bfloat16 [128, 512], replicated, may hold values from -0.5 to 0.5
- col_bias_proj: bfloat16 [128, 4], replicated, may hold values from -36 to 36
- col_output: bfloat16 [128, 128], replicated, may hold values from -0.5 to 0.5
- tri_left: bfloat16 [128, 256], replicated, may hold values from -0.5 to 0.5
- tri_right: bfloat16 [128, 256], replicated, may hold values from -0.5 to 0.5
- tri_gate: bfloat16 [128, 128], replicated, may hold values from -0.5 to 0.5
- tri_output: bfloat16 [128, 128], replicated, may hold values from -1.5 to 1.5
Outputs:
- pair_out: bfloat16 [512, 512, 128], P('row', 'col')
Inputs may be any that keep to these rules, and one draw needn't show every extreme that they name: `tile_mask`: every diagonal entry is 1. `chain_ids`: chain numbers never fall along the residues.
All inputs are finite; a program needn't handle non-finite values.
Results may differ from a plain program's by a relative error of at most 0.018.
Values may be sent and summed in bfloat16 or wider, within the bound.
A program may use at most 64 MiB of HBM per device.

v0:
```python
import jax
import jax.numpy as jnp
from jax import lax
from jax.sharding import PartitionSpec as P


def layer_norm(values):
    values = values.astype(jnp.float32)
    center = values - jnp.mean(values, axis=-1, keepdims=True)
    spread = jnp.mean(center * center, axis=-1, keepdims=True)
    return center * lax.rsqrt(spread + 1e-05)


def tile_rows(positions, tile_table, length):
    tile_count = tile_table.shape[0]
    tile_width = length // tile_count
    onehot = (positions[:, None] // tile_width == jnp.arange(tile_count)[None, :]).astype(
        jnp.float32
    )
    picked = jnp.dot(onehot, tile_table.astype(jnp.float32))
    spread_out = jnp.broadcast_to(picked[:, :, None], (positions.shape[0], tile_count, tile_width))
    return spread_out.reshape(positions.shape[0], length) > 0.5


def tile_pairs(row_pos, col_pos, tile_table, length):
    tile_count = tile_table.shape[0]
    tile_width = length // tile_count
    row_hot = (row_pos[:, None] // tile_width == jnp.arange(tile_count)[None, :]).astype(
        jnp.float32
    )
    col_hot = (col_pos[:, None] // tile_width == jnp.arange(tile_count)[None, :]).astype(
        jnp.float32
    )
    return jnp.dot(jnp.dot(row_hot, tile_table.astype(jnp.float32)), col_hot.T)


def attend_lines(
    queries,
    key_rows,
    value_rows,
    gate_pre,
    bias_all,
    key_ok,
    chain_ids,
    chain_add,
    line_dim,
    flipped,
):
    line_count = queries.shape[line_dim]
    length = queries.shape[1 - line_dim]
    head_count = queries.shape[2]
    head_size = queries.shape[3]
    width_all = head_count * head_size
    query_rows = min(128, length)
    per_line = length // query_rows
    scaling = head_size ** (-0.5)

    def one_block(block_index):
        line_index = block_index // per_line
        offset = block_index % per_line * query_rows
        query_line = lax.dynamic_index_in_dim(queries, line_index, line_dim, keepdims=False)
        query_block = lax.dynamic_slice_in_dim(query_line, offset, query_rows, 0)
        key_line = lax.dynamic_index_in_dim(key_rows, line_index, line_dim, keepdims=False)
        value_line = lax.dynamic_index_in_dim(value_rows, line_index, line_dim, keepdims=False)
        scores = (
            jnp.einsum("qhd,khd->hqk", query_block, key_line, preferred_element_type=jnp.float32)
            * scaling
        )
        if flipped:
            bias_block = lax.dynamic_slice_in_dim(bias_all, offset, query_rows, 2).transpose(
                0, 2, 1
            )
        else:
            bias_block = lax.dynamic_slice_in_dim(bias_all, offset, query_rows, 1)
        scores = scores + bias_block
        chain_block = lax.dynamic_slice_in_dim(chain_ids, offset, query_rows, 0)
        same_chain = (chain_block[:, None] == chain_ids[None, :]).astype(jnp.float32)
        scores = scores + chain_add[:, None, None] * same_chain[None]
        usable = lax.dynamic_index_in_dim(key_ok, line_index, 0, keepdims=False)
        scores = jnp.where(usable[None, None, :], scores, -1000000000.0)
        row_peak = jnp.max(scores, axis=-1, keepdims=True)
        weights = jnp.exp(scores - row_peak)
        attention = (weights / jnp.sum(weights, axis=-1, keepdims=True)).astype(jnp.bfloat16)
        mixed_rows = jnp.einsum(
            "hqk,khd->qhd", attention, value_line, preferred_element_type=jnp.float32
        ).reshape(query_rows, width_all)
        gate_line = lax.dynamic_index_in_dim(gate_pre, line_index, line_dim, keepdims=False)
        gate_block = lax.dynamic_slice_in_dim(gate_line, offset, query_rows, 0)
        return (mixed_rows * jax.nn.sigmoid(gate_block)).astype(jnp.bfloat16)

    outputs = lax.map(one_block, jnp.arange(line_count * per_line, dtype=jnp.int32))
    outputs = outputs.reshape(line_count, length, width_all)
    if line_dim == 1:
        outputs = outputs.transpose(1, 0, 2)
    return outputs


def tri_acts(normed, weights, allowed):
    channels = normed.shape[-1]
    projected = jnp.dot(normed.reshape(-1, channels), weights, preferred_element_type=jnp.float32)
    projected = projected.reshape(normed.shape[0], normed.shape[1], 2 * channels)
    return (
        jax.nn.sigmoid(projected[..., channels:]) * projected[..., :channels] * allowed[..., None]
    ).astype(jnp.bfloat16)


def shards(
    pair_rep,
    tile_mask,
    chain_ids,
    chain_bias,
    row_project,
    row_bias_proj,
    row_output,
    col_project,
    col_bias_proj,
    col_output,
    tri_left,
    tri_right,
    tri_gate,
    tri_output,
):
    n_row = lax.axis_size("row")
    n_col = lax.axis_size("col")
    device_count = n_row * n_col
    rows_here, length, channels = pair_rep.shape
    head_count = row_bias_proj.shape[1]
    head_size = channels // head_count
    row_index = lax.axis_index("row")
    col_index = lax.axis_index("col")
    device_index = row_index * n_col + col_index
    local_lines = device_index * rows_here + jnp.arange(rows_here, dtype=jnp.int32)
    normed = layer_norm(pair_rep).astype(jnp.bfloat16)
    flat_rows = normed.reshape(rows_here * length, channels)
    bias_rows = jnp.dot(flat_rows, row_bias_proj, preferred_element_type=jnp.float32)
    bias_rows = bias_rows.reshape(rows_here, length, head_count).transpose(2, 0, 1)
    bias_all = lax.all_gather(bias_rows, ("row", "col"), axis=1, tiled=True)
    projected = jnp.dot(flat_rows, row_project, preferred_element_type=jnp.float32).reshape(
        rows_here, length, 4 * channels
    )
    qkv_rows = (
        projected[..., : 3 * channels]
        .astype(jnp.bfloat16)
        .reshape(rows_here, length, 3, head_count, head_size)
    )
    key_ok = tile_rows(local_lines, tile_mask, length)
    mixed_rows = attend_lines(
        qkv_rows[:, :, 0],
        qkv_rows[:, :, 1],
        qkv_rows[:, :, 2],
        projected[..., 3 * channels :],
        bias_all,
        key_ok,
        chain_ids,
        chain_bias[0],
        0,
        False,
    )
    update = jnp.dot(
        mixed_rows.reshape(-1, channels), row_output, preferred_element_type=jnp.float32
    ).reshape(rows_here, length, channels)
    first_pair = (pair_rep.astype(jnp.float32) + update).astype(jnp.bfloat16)
    normed_first = layer_norm(first_pair).astype(jnp.bfloat16)
    bias_next = jnp.dot(
        normed_first.reshape(-1, channels), col_bias_proj, preferred_element_type=jnp.float32
    )
    bias_next = bias_next.reshape(rows_here, length, head_count).transpose(2, 0, 1)
    bias_cols = lax.all_gather(bias_next, ("row", "col"), axis=1, tiled=True)
    columns = lax.all_to_all(first_pair, ("row", "col"), split_axis=1, concat_axis=0, tiled=True)
    normed_cols = layer_norm(columns).astype(jnp.bfloat16)
    projected_cols = jnp.dot(
        normed_cols.reshape(-1, channels), col_project, preferred_element_type=jnp.float32
    ).reshape(length, rows_here, 4 * channels)
    qkv_cols = (
        projected_cols[..., : 3 * channels]
        .astype(jnp.bfloat16)
        .reshape(length, rows_here, 3, head_count, head_size)
    )
    col_ok = tile_rows(local_lines, tile_mask.T, length)
    mixed_cols = attend_lines(
        qkv_cols[:, :, 0],
        qkv_cols[:, :, 1],
        qkv_cols[:, :, 2],
        projected_cols[..., 3 * channels :],
        bias_cols,
        col_ok,
        chain_ids,
        chain_bias[1],
        1,
        True,
    )
    update_cols = jnp.dot(
        mixed_cols.reshape(-1, channels), col_output, preferred_element_type=jnp.float32
    ).reshape(length, rows_here, channels)
    second_pair = (columns.astype(jnp.float32) + update_cols).astype(jnp.bfloat16)
    normed_second = layer_norm(second_pair).astype(jnp.bfloat16)
    edge_mask = tile_pairs(jnp.arange(length, dtype=jnp.int32), local_lines, tile_mask, length)
    left_all = tri_acts(normed_second, tri_left, edge_mask)
    right_all = tri_acts(normed_second, tri_right, edge_mask)
    block_rows = length // n_row
    block_cols = length // n_col

    def one_round(round_index, loop_state):
        product_sum, own_block = loop_state
        left_col = lax.dynamic_index_in_dim(left_all, round_index, 1, keepdims=False)
        right_col = lax.dynamic_index_in_dim(right_all, round_index, 1, keepdims=False)
        raw_col = lax.dynamic_index_in_dim(second_pair, round_index, 1, keepdims=False)
        left_send = jnp.broadcast_to(
            left_col.reshape(n_row, 1, block_rows, channels), (n_row, n_col, block_rows, channels)
        )
        raw_send = jnp.broadcast_to(
            raw_col.reshape(n_row, 1, block_rows, channels), (n_row, n_col, block_rows, channels)
        )
        right_send = jnp.broadcast_to(
            right_col.reshape(1, n_col, block_cols, channels), (n_row, n_col, block_cols, channels)
        )
        outgoing = jnp.concatenate([left_send, raw_send, right_send], axis=2).reshape(
            device_count, 2 * block_rows + block_cols, channels
        )
        received = lax.all_to_all(outgoing, ("row", "col"), split_axis=0, concat_axis=0, tiled=True)
        left_act = received[:, :block_rows].transpose(1, 0, 2)
        right_act = received[:, 2 * block_rows :].transpose(1, 0, 2)
        product_sum = product_sum + jnp.einsum(
            "ikc,jkc->ijc", left_act, right_act, preferred_element_type=jnp.float32
        )
        own_piece = lax.dynamic_slice_in_dim(
            received[:, block_rows : 2 * block_rows], col_index * n_row, n_row, 0
        )
        own_block = lax.dynamic_update_index_in_dim(own_block, own_piece, round_index, 1)
        return (product_sum, own_block)

    initial = (
        jnp.zeros((block_rows, block_cols, channels), jnp.float32),
        jnp.zeros((n_row, rows_here, block_rows, channels), jnp.bfloat16),
    )
    product_sum, own_block = lax.fori_loop(0, rows_here, one_round, initial)
    own_pair = own_block.transpose(2, 0, 1, 3).reshape(block_rows, block_cols, channels)
    normed_own = layer_norm(own_pair).astype(jnp.bfloat16)
    gate_values = jax.nn.sigmoid(
        jnp.dot(normed_own.reshape(-1, channels), tri_gate, preferred_element_type=jnp.float32)
    ).reshape(block_rows, block_cols, channels)
    centered = layer_norm(product_sum).astype(jnp.bfloat16)
    update_tri = jnp.dot(
        centered.reshape(-1, channels), tri_output, preferred_element_type=jnp.float32
    ).reshape(block_rows, block_cols, channels)
    return (own_pair.astype(jnp.float32) + gate_values * update_tri).astype(jnp.bfloat16)


def solution(mesh):
    return jax.shard_map(
        shards,
        mesh=mesh,
        in_specs=(
            P(("row", "col"), None, None),
            P(),
            P(),
            P(),
            P(),
            P(),
            P(),
            P(),
            P(),
            P(),
            P(),
            P(),
            P(),
            P(),
        ),
        out_specs=P("row", "col", None),
        check_vma=False,
    )
```

profile of v0, /device:TPU:1, one launch (start us, length us, event | category | flops | bytes accessed | tf_op | source)
XLA Modules:
  0.0 913.0 jit_solution(16017339999613276944)
XLA Ops:
  13.8 67.3 %all-gather.3.cloned.1.call-done = f32[4,512,512]{2,0,1:T(4,128)} async-done(((f32[4,4,512]{2,0,1:T(4,128)}), f32[4,512,512]{2,0,1:T(4,128)}) %all-gather.3.cloned.1.call-update) | async-done | bytes 4194320 | tf_op jit(solution)/shard_map/all_gather | solution.py:137
  82.0 164.6 %while.44 = (s32[]{:T(128)}, bf16[16,128,128]{2,1,0:T(8,128)(2,1)}, s32[16]{0:T(128)S(1)}, bf16[4,512,4,32]{1,3,2,0:T(8,128)(2,1)}, pred[4,512]{1,0:T(4,128)(4,1...) while((s32[]{:T(128)}, bf16[16,128,128]{2,1,0:T(8,128)(2,1)}, ...), condition=%wide.region_5.6_spmd, body=%wide.region_2.5_spmd.sunk | while | flops 36390428 | bytes 8530448 | solution.py:91
  250.4 5.3 all-to-all-start.1
  256.7 12.8 %all-to-all-done.1 = bf16[4,512,128]{2,0,1:T(4,128)(2,1)S(1)} async-done(((bf16[4,512,128]{2,0,1:T(4,128)(2,1)}), bf16[4,512,128]{2,0,1:T(4,128)(2,1)S(1)}, u32[]{:S(2)}, u32[]{:S(2)}) %all-to-all-start.1) | async-done | bytes 524320 | tf_op jit(solution)/shard_map/all_to_all | solution.py:169
  275.4 2.9 fusion.74
  282.1 2.6 slice_bitcast_fusion
  284.7 31.5 %all-gather.5.cloned.1.call-done = f32[4,512,512]{2,0,1:T(4,128)} async-done(((f32[4,4,512]{2,0,1:T(4,128)}), f32[4,512,512]{2,0,1:T(4,128)}) %all-gather.5.cloned.1.call-update) | async-done | bytes 4194320 | tf_op jit(solution)/shard_map/all_gather | solution.py:168
  317.1 228.6 %while.45 = (s32[]{:T(128)}, bf16[16,128,128]{2,1,0:T(8,128)(2,1)}, s32[16]{0:T(128)S(1)}, bf16[512,4,4,32]{0,3,2,1:T(8,128)(2,1)}, pred[4,512]{1,0:T(4,128)(4,1...) while((s32[]{:T(128)}, bf16[16,128,128]{2,1,0:T(8,128)(2,1)}, ...), condition=%wide.region_13.14_spmd, body=%wide.region_10.13_spmd.sunk | while | flops 36390428 | bytes 14821436 | solution.py:91
  319.6 2.3 constant_dynamic-slice_fusion.10
  327.0 2.6 fusion.160
  333.9 2.3 constant_dynamic-slice_fusion.10
  341.3 2.6 fusion.160
  348.3 2.3 constant_dynamic-slice_fusion.10
  355.7 2.6 fusion.160
  362.6 2.3 constant_dynamic-slice_fusion.10
  369.9 2.6 fusion.160
  376.8 2.3 constant_dynamic-slice_fusion.10
  384.2 2.6 fusion.160
  391.1 2.3 constant_dynamic-slice_fusion.10
  398.5 2.6 fusion.160
  405.4 2.3 constant_dynamic-slice_fusion.10
  412.8 2.6 fusion.160
  419.7 2.3 constant_dynamic-slice_fusion.10
  427.1 2.6 fusion.160
  433.9 2.3 constant_dynamic-slice_fusion.10
  441.3 2.6 fusion.160
  448.2 2.3 constant_dynamic-slice_fusion.10
  455.6 2.6 fusion.160
  462.6 2.3 constant_dynamic-slice_fusion.10
  470.0 2.6 fusion.160
  476.9 2.3 constant_dynamic-slice_fusion.10
  484.3 2.6 fusion.160
  491.1 2.3 constant_dynamic-slice_fusion.10
  498.5 2.6 fusion.160
  512.8 2.6 fusion.160
  519.7 2.3 constant_dynamic-slice_fusion.10
  527.1 2.6 fusion.160
  541.4 2.6 fusion.160
  550.4 341.5 %while.46 = (s32[]{:T(128)}, f32[32,64,128]{1,0,2:T(8,128)S(1)}, bf16[16,4,32,128]{3,0,1,2:T(8,128)(2,1)}, bf16[512,4,128]{2,0,1:T(8,128)(2,1)}, bf16[512,4,128]...) while((s32[]{:T(128)}, f32[32,64,128]{1,0,2:T(8,128)S(1)}, ...), condition=%wide.region_17.18_spmd.clone, body=%wide.region_16.17_spmd.clone.sunk | while | flops 80216064 | bytes 53608632 | solution.py:236
  554.5 6.4 copy.270
  560.9 5.8 all-to-all-start
  566.7 52.8 %all-to-all-done = bf16[128,128,128]{1,2,0:T(8,128)(2,1)} async-done(((bf16[128,128,128]{1,2,0:T(8,128)(2,1)}), bf16[128,128,128]{1,2,0:T(8,128)(2,1)}, u32[]{:S(2)}, u32[]{:S(2)}) %all-to-all-start) | async-done | bytes 4194336 | tf_op jit(solution)/shard_map/while/body/eval_jaxpr/all_to_all | solution.py:220
  619.5 6.7 fusion.164
  627.1 3.6 slice.160
  630.7 5.0 bitcast_add_fusion.2
  639.8 6.4 copy.270
  646.2 5.7 all-to-all-start
  651.9 52.9 %all-to-all-done = bf16[128,128,128]{1,2,0:T(8,128)(2,1)} async-done(((bf16[128,128,128]{1,2,0:T(8,128)(2,1)}), bf16[128,128,128]{1,2,0:T(8,128)(2,1)}, u32[]{:S(2)}, u32[]{:S(2)}) %all-to-all-start) | async-done | bytes 4194336 | tf_op jit(solution)/shard_map/while/body/eval_jaxpr/all_to_all | solution.py:220
  704.8 6.7 fusion.164
  712.4 3.6 slice.160
  716.0 5.0 bitcast_add_fusion.2
  725.2 6.4 copy.270
  731.5 5.8 all-to-all-start
  737.3 52.8 %all-to-all-done = bf16[128,128,128]{1,2,0:T(8,128)(2,1)} async-done(((bf16[128,128,128]{1,2,0:T(8,128)(2,1)}), bf16[128,128,128]{1,2,0:T(8,128)(2,1)}, u32[]{:S(2)}, u32[]{:S(2)}) %all-to-all-start) | async-done | bytes 4194336 | tf_op jit(solution)/shard_map/while/body/eval_jaxpr/all_to_all | solution.py:220
  790.1 6.7 fusion.164
  797.7 3.6 slice.160
  801.3 5.0 bitcast_add_fusion.2
  810.5 6.4 copy.270
  816.8 5.8 all-to-all-start
  822.6 52.8 %all-to-all-done = bf16[128,128,128]{1,2,0:T(8,128)(2,1)} async-done(((bf16[128,128,128]{1,2,0:T(8,128)(2,1)}), bf16[128,128,128]{1,2,0:T(8,128)(2,1)}, u32[]{:S(2)}, u32[]{:S(2)}) %all-to-all-start) | async-done | bytes 4194336 | tf_op jit(solution)/shard_map/while/body/eval_jaxpr/all_to_all | solution.py:220
  875.4 6.7 fusion.164
  883.1 3.6 slice.160
  886.7 5.0 bitcast_add_fusion.2
  903.1 3.0 fusion.45
  (529 shorter events, 294.7 us)
Async XLA Ops:
  6.5 3.2 copy-start
  6.5 74.6 %all-gather.3.cloned.1.call-start = ((), (), s32[]{:S(2)}) async-start(), calls=%async_computation.2 | async-start | bytes 4227072 | tf_op jit(solution)/shard_map/all_gather | solution.py:137
  9.7 2.1 copy-start.17
  9.7 2.4 copy-start.15
  9.7 306.5 %all-gather.5.cloned.1.call-start = ((), (), s32[]{:S(2)}) async-start(), calls=%async_computation.3 | async-start | bytes 4227072 | tf_op jit(solution)/shard_map/all_gather | solution.py:168
  10.5 71.5 %copy-start.6 = (s32[512]{0:T(512)S(1)}, s32[512]{0:T(512)}, u32[]{:S(2)}) copy-start(s32[512]{0:T(512)} %param.22) | copy-start | bytes 6148
  82.0 164.6 %copy-start.12 = (bf16[128,128]{1,0:T(8,128)(2,1)S(1)}, bf16[128,128]{1,0:T(8,128)(2,1)}, u32[]{:S(2)}) copy-start(bf16[128,128]{1,0:T(8,128)(2,1)} %param.26) | copy-start | bytes 98308
  82.0 166.2 %copy-start.18 = (bf16[128,4]{0,1:T(4,128)(2,1)S(1)}, bf16[128,4]{0,1:T(4,128)(2,1)}, u32[]{:S(2)}) copy-start(bf16[128,4]{0,1:T(4,128)(2,1)} %param.28) | copy-start | bytes 3076
  250.4 19.2 %all-to-all-start.1 = ((bf16[4,512,128]{2,0,1:T(4,128)(2,1)}), bf16[4,512,128]{2,0,1:T(4,128)(2,1)S(1)}, u32[]{:S(2)}, u32[]{:S(2)}) async-start(bf16[4,512,128]{2,0,1:T(4,128)(2,1)} %copy.166), calls=%async_computation.1 | async-start | bytes 1048576 | tf_op jit(solution)/shard_map/all_to_all | solution.py:169
  269.7 5.8 copy-start.7
  279.7 37.4 %copy-start.13 = (f32[1,4]{1,0:T(1,128)S(1)}, f32[1,4]{1,0:T(1,128)}, u32[]{:S(2)}) copy-start(f32[1,4]{1,0:T(1,128)} %get-tuple-element.1039) | copy-start | bytes 52
  317.1 228.6 %copy-start.10 = (bf16[128,128]{1,0:T(8,128)(2,1)S(1)}, bf16[128,128]{1,0:T(8,128)(2,1)}, u32[]{:S(2)}) copy-start(bf16[128,128]{1,0:T(8,128)(2,1)} %param.29) | copy-start | bytes 98308
  317.1 230.6 %copy-start.8 = (bf16[128,256]{1,0:T(8,128)(2,1)S(1)}, bf16[128,256]{1,0:T(8,128)(2,1)}, u32[]{:S(2)}) copy-start(bf16[128,256]{1,0:T(8,128)(2,1)} %param.30) | copy-start | bytes 196612
  325.8 1.0 copy-start.3
  340.1 1.0 copy-start.3
  354.4 1.0 copy-start.3
  368.7 1.0 copy-start.3
  382.9 1.0 copy-start.3
  397.2 1.0 copy-start.3
  411.5 1.0 copy-start.3
  425.8 1.0 copy-start.3
  440.0 1.0 copy-start.3
  454.4 1.0 copy-start.3
  468.7 1.0 copy-start.3
  483.0 1.0 copy-start.3
  497.2 1.0 copy-start.3
  511.6 1.0 copy-start.3
  525.9 1.0 copy-start.3
  540.1 1.0 copy-start.3
  545.8 2.5 copy-start.9
  545.8 3.0 copy-start.14
  560.9 58.6 %all-to-all-start = ((bf16[128,128,128]{1,2,0:T(8,128)(2,1)}), bf16[128,128,128]{1,2,0:T(8,128)(2,1)}, u32[]{:S(2)}, u32[]{:S(2)}) async-start(bf16[128,128,128]{1,2,0:T(8,128)(2,1)} %copy.270), calls=%async_computation | async-start | bytes 8388608 | tf_op jit(solution)/shard_map/while/body/eval_jaxpr/all_to_all | solution.py:220
  627.1 3.6 copy-start.2
  646.2 58.6 %all-to-all-start = ((bf16[128,128,128]{1,2,0:T(8,128)(2,1)}), bf16[128,128,128]{1,2,0:T(8,128)(2,1)}, u32[]{:S(2)}, u32[]{:S(2)}) async-start(bf16[128,128,128]{1,2,0:T(8,128)(2,1)} %copy.270), calls=%async_computation | async-start | bytes 8388608 | tf_op jit(solution)/shard_map/while/body/eval_jaxpr/all_to_all | solution.py:220
  712.4 3.6 copy-start.2
  731.5 58.6 %all-to-all-start = ((bf16[128,128,128]{1,2,0:T(8,128)(2,1)}), bf16[128,128,128]{1,2,0:T(8,128)(2,1)}, u32[]{:S(2)}, u32[]{:S(2)}) async-start(bf16[128,128,128]{1,2,0:T(8,128)(2,1)} %copy.270), calls=%async_computation | async-start | bytes 8388608 | tf_op jit(solution)/shard_map/while/body/eval_jaxpr/all_to_all | solution.py:220
  797.7 3.6 copy-start.2
  816.8 58.6 %all-to-all-start = ((bf16[128,128,128]{1,2,0:T(8,128)(2,1)}), bf16[128,128,128]{1,2,0:T(8,128)(2,1)}, u32[]{:S(2)}, u32[]{:S(2)}) async-start(bf16[128,128,128]{1,2,0:T(8,128)(2,1)} %copy.270), calls=%async_computation | async-start | bytes 8388608 | tf_op jit(solution)/shard_map/while/body/eval_jaxpr/all_to_all | solution.py:220
  883.1 3.6 copy-start.2
  897.9 1.8 copy-start.4
  897.9 3.2 copy-start.16
  898.4 4.7 copy-start.11
  899.7 3.4 copy-start.5
  901.0 5.1 copy-start.1
Sparse Core Ops, SparseCore 0:
  10.5 70.5 all-gather.2
  249.2 66.9 all-gather.4
where the time goes:
time: 920 us; the launch traced here: 913 us
  waiting for transfers between devices  323 us (35%)
  local copies, waits for them, and re-layouts  243 us (26%)
  matrix products  157 us (17%)
  loops' own time  84.4 us (9%)
  other arithmetic  63 us (7%)
  starting transfers between devices  28.3 us (3%)
  between operations  13.8 us (2%)
    all_to_all x4, waiting for transfers between devices, one_round(): lax.all_to_all(outgoing, ('row', 'col'), split_axis=0, concat_axis=0, til...  211 us
    another operation x2, loops' own time, attend_lines(): lax.map(one_block, jnp.arange(line_count * per_line, dtype=jnp.int32))  83.8 us
    dot_general x32, matrix products, one_block(): jnp.einsum('hqk,khd->qhd', attention, value_line, preferred_element_type=...  73.4 us
    all_gather x1, waiting for transfers between devices, shards(): bias_all = lax.all_gather(bias_rows, ('row', 'col'), axis=1, tiled=True)  67.3 us
    dynamic_slice x32, local copies, waits for them, and re-layouts, one_block(): lax.dynamic_slice_in_dim(bias_all, offset, query_rows, 2).transpose(0, 2, 1)  61.2 us
    dot_general x32, matrix products, one_block(): jnp.einsum('qhd,khd->hqk', query_block, key_line, preferred_element_type=...  47.5 us
    convert_element_type x32, other arithmetic, one_block(): return (mixed_rows * jax.nn.sigmoid(gate_block)).astype(jnp.bfloat16)  32.6 us
    all_gather x1, waiting for transfers between devices, shards(): bias_cols = lax.all_gather(bias_next, ('row', 'col'), axis=1, tiled=True)  31.5 us
  transfers between devices with their start and end apart: 7, of which 7 were waited for; matrix products, arithmetic and copies ran while one was open for 2% of the time, Pallas kernels for 0%

commit v1 on v0

v1 whole, which is shorter than its diff:
```python
import functools
import math

import jax
import jax.numpy as jnp
from jax import lax
from jax.experimental import pallas as pl
from jax.experimental.pallas import tpu as pltpu
from jax.sharding import PartitionSpec as P

MESH = pl.DeviceIdType.MESH
F32 = jnp.float32
BF16 = jnp.bfloat16
DEVS = 128
LOG2E = 1.4426950408889634
VMEM_LIMIT = 50 * 2**20


def vmem():
    return pl.BlockSpec(memory_space=pltpu.VMEM)


def smem():
    return pl.BlockSpec(memory_space=pltpu.SMEM)


def layer_norm(values):
    center = values - jnp.mean(values, axis=-1, keepdims=True)
    spread = jnp.mean(center * center, axis=-1, keepdims=True)
    return center * lax.rsqrt(spread + 1e-05)


def dot(a, b, ca=1, cb=0):
    return lax.dot_general(a, b, (((ca,), (cb,)), ((), ())), preferred_element_type=F32)


def sigmoid(x):
    return 1.0 / (1.0 + jnp.exp(-x))


def my_place():
    row, col = lax.axis_index("row"), lax.axis_index("col")
    return row, col, row * 8 + col


def drain(ref, sem):
    pltpu.make_async_copy(ref, ref, sem).wait()


def write_bias_block(blk_ref, line, bias):
    for half in range(2):
        for tile in range(4):
            blk_ref[half, tile, 2 * line : 2 * line + 2, :] = bias[
                2 * half : 2 * half + 2, tile * 128 : (tile + 1) * 128
            ]


def greet(partners):
    barrier = pltpu.get_barrier_semaphore()
    for partner in partners:
        pl.semaphore_signal(barrier, inc=1, device_id=partner, device_id_type=MESH)
    pl.semaphore_wait(barrier, len(partners))


def gather_partners():
    row, col, _ = my_place()
    core, z, y, x = col % 2, col // 2, row % 4, row // 4
    sibling = (row, z * 2 + 1 - core)
    partners = [sibling]
    for step in (1, 2, 3):
        partners.append((row, (z + step) % 4 * 2 + core))
        partners.append((x * 4 + (y + step) % 4, col))
        partners.append(((x + step) % 4 * 4 + y, col))
    return partners


def gather_bias(blk_ref, g_ref, own_sem, zs, zr, as_, ar_, bs, br, fs, fr):
    row, col, dev = my_place()
    core, z, y, x = col % 2, col // 2, row % 4, row // 4
    a_me = jnp.where(core == 0, y, x)
    b_me = jnp.where(core == 0, x, y)
    sibling = (row, z * 2 + 1 - core)

    def row_of(a, b):
        a, b = lax.rem(a, 4), lax.rem(b, 4)
        return jnp.where(core == 0, b * 4 + a, a * 4 + b)

    def part(half, start, size):
        return g_ref.at[half, :, pl.ds(pl.multiple_of(start, 8), size), :]

    started = []

    def send(src, dst, ssem, rsem, device):
        copy = pltpu.make_async_remote_copy(
            src_ref=src, dst_ref=dst, send_sem=ssem, recv_sem=rsem, device_id=device, device_id_type=MESH
        )
        copy.start()
        started.append(copy)

    def arrived(ref, sem):
        drain(ref, sem)

    own = pltpu.make_async_copy(blk_ref.at[core], part(core, dev * 8, 8), own_sem.at[0])
    own.start()
    send(blk_ref.at[1 - core], part(1 - core, dev * 8, 8), own_sem.at[1], own_sem.at[2], sibling)
    own.wait()
    sib_dev = row * 8 + z * 2 + 1 - core
    arrived(part(core, sib_dev * 8, 8), own_sem.at[2])

    chip = part(core, (row * 8 + z * 2) * 8, 16)
    for step in (1, 3, 2):
        send(chip, chip, zs.at[step], zr.at[4 - step], (row, lax.rem(z + step, 4) * 2 + core))
    for step in (1, 3, 2):
        arrived(part(core, (row * 8 + lax.rem(z + step, 4) * 2) * 8, 16), zr.at[step])

    def block(da, db):
        return part(core, row_of(a_me + da, b_me + db) * 64, 64)

    def to_sibling(da, db):
        ref = block(da, db)
        send(ref, ref, fs.at[da * 4 + db], fr.at[da * 4 + db], sibling)

    def along_b(da, db, step):
        ref = block(da, db)
        rel = (db - step) % 4
        send(ref, ref, bs.at[da * 4 + rel], br.at[da * 4 + rel], (row_of(a_me, b_me + step), col))

    for step in (1, 3, 2):
        ref = block(0, 0)
        send(ref, ref, as_.at[step], ar_.at[4 - step], (row_of(a_me + step, b_me), col))
    along_b(0, 0, 1)
    along_b(0, 0, 3)
    to_sibling(0, 0)
    for da in (1, 3, 2):
        arrived(block(da, 0), ar_.at[da])
        along_b(da, 0, 1)
        along_b(da, 0, 3)
        to_sibling(da, 0)
    for da in (0, 1, 3, 2):
        arrived(block(da, 3), br.at[da * 4 + 3])
        if da in (0, 3):
            along_b(da, 3, 1)
        to_sibling(da, 3)
        arrived(block(da, 1), br.at[da * 4 + 1])
        if da in (1, 2):
            along_b(da, 1, 3)
        to_sibling(da, 1)
    for da in (0, 1, 3, 2):
        arrived(block(da, 2), br.at[da * 4 + 2])
        to_sibling(da, 2)

    def finish():
        for da in range(4):
            for db in range(4):
                s_row = jnp.where(
                    core == 1,
                    lax.rem(x + db, 4) * 4 + lax.rem(y + da, 4),
                    lax.rem(x + da, 4) * 4 + lax.rem(y + db, 4),
                )
                arrived(part(1 - core, s_row * 64, 64), fr.at[da * 4 + db])
        for copy in started:
            copy.wait_send()

    return finish


GATHER_SEMS = [pltpu.SemaphoreType.DMA((n,)) for n in (3, 4, 4, 4, 4, 16, 16, 16, 16)]
G_SHAPE = (2, 4, 1024, 128)


def start_kernel(x_ref, bias_w_ref, g_ref, blk, *sems):
    for line in range(4):
        normed = layer_norm(x_ref[line].astype(F32)).astype(BF16)
        write_bias_block(blk, line, dot(bias_w_ref[...], normed, 0, 1))
    greet(gather_partners())
    gather_bias(blk, g_ref, *sems)()


def start(x, bias_w):
    return pl.pallas_call(
        start_kernel,
        out_shape=jax.ShapeDtypeStruct(G_SHAPE, F32),
        in_specs=[vmem(), vmem()],
        out_specs=vmem(),
        scratch_shapes=[pltpu.VMEM((2, 4, 8, 128), F32)] + GATHER_SEMS,
        compiler_params=pltpu.CompilerParams(
            collective_id=0, has_side_effects=True, vmem_limit_bytes=VMEM_LIMIT
        ),
        name="bias_gather",
    )(x, bias_w)


def all_to_all_start(src_ref, dst_ref, ssem, rsem, lsem):
    row, col, dev = my_place()
    pltpu.make_async_copy(src_ref.at[dev], dst_ref.at[dev], lsem).start()

    def step(off, carry):
        dest = lax.rem(dev + off, DEVS)
        pltpu.make_async_remote_copy(
            src_ref=src_ref.at[dest],
            dst_ref=dst_ref.at[dev],
            send_sem=ssem,
            recv_sem=rsem,
            device_id=(dest // 8, dest % 8),
            device_id_type=MESH,
        ).start()
        return carry

    lax.fori_loop(1, DEVS, step, 0)


def all_to_all_recv(src_ref, dst_ref, ssem, rsem, lsem):
    rest = dst_ref.at[pl.ds(0, DEVS - 1)]
    drain(dst_ref.at[0], lsem)
    drain(rest, rsem)


def all_to_all_sent(src_ref, dst_ref, ssem, rsem, lsem):
    drain(src_ref.at[pl.ds(0, DEVS - 1)], ssem)


def greet_all():
    _, _, dev = my_place()
    barrier = pltpu.get_barrier_semaphore()

    def step(off, carry):
        dest = lax.rem(dev + off, DEVS)
        pl.semaphore_signal(barrier, inc=1, device_id=(dest // 8, dest % 8), device_id_type=MESH)
        return carry

    lax.fori_loop(1, DEVS, step, 0)
    pl.semaphore_wait(barrier, DEVS - 1)


def middle_kernel(blk_ref, pair_ref, g_ref, cols_ref, s0, s1, s2, *sems):
    greet_all()
    args = (pair_ref, cols_ref, s0, s1, s2)
    all_to_all_start(*args)
    finish = gather_bias(blk_ref, g_ref, *sems)
    finish()
    all_to_all_recv(*args)
    all_to_all_sent(*args)


def middle(blk, pair):
    return pl.pallas_call(
        middle_kernel,
        out_shape=(jax.ShapeDtypeStruct(G_SHAPE, F32), jax.ShapeDtypeStruct((128, 16, 128), BF16)),
        in_specs=[vmem(), vmem()],
        out_specs=(vmem(), vmem()),
        scratch_shapes=[pltpu.SemaphoreType.DMA] * 3 + GATHER_SEMS,
        compiler_params=pltpu.CompilerParams(
            collective_id=1, has_side_effects=True, vmem_limit_bytes=VMEM_LIMIT
        ),
        name="columns_and_bias",
    )(blk, pair)


def compact(flags):
    count = jnp.int32(0)
    picked = [jnp.int32(0)] * 4
    for tile in range(4):
        for place in range(4):
            hit = jnp.logical_and(flags[tile] > 0, count == place)
            picked[place] = jnp.where(hit, tile, picked[place])
        count = count + flags[tile]
    return picked, count


def attention(
    first, lines, flags, g_ref, ids_ref, chain_add, project_ref, output_ref, emit, k_buf, q_buf, v_buf, gate_buf, mix_buf, ids_buf
):
    scale = LOG2E * 32 ** (-0.5)
    w_k = project_ref[:, 128:256]
    w_q = project_ref[:, 0:128]
    w_vg = project_ref[:, 256:512]
    for line in range(4):
        normed = layer_norm(lines(line)).astype(BF16)
        k_buf[line] = dot(normed, w_k).astype(BF16)
        q_buf[line] = dot(w_q, normed, 0, 1).astype(BF16)
        vg = dot(w_vg, normed, 0, 1)
        v_buf[line] = vg[:128].astype(BF16)
        gate_buf[line] = sigmoid(vg[128:])
    ids = ids_ref[...].astype(F32)
    for tile in range(4):
        ids_buf[tile] = jnp.broadcast_to(ids[:, tile * 128 : (tile + 1) * 128], (128, 128)).T
    picked, count = compact(flags)

    def run(tiles):
        def body(step, carry):
            head, block = step // 2, step % 2
            half, sub = head // 2, head % 2
            q_at = pl.ds(pl.multiple_of(block * 256, 256), 256)
            head_at = pl.ds(pl.multiple_of(head * 32, 32), 32)
            head_mask = jnp.where(lax.broadcasted_iota(jnp.int32, (1, 128), 1) // 32 == head, 1.0, 0.0).astype(BF16)
            add = chain_add(head)
            q_ids = jnp.concatenate([ids_ref[:, pl.ds(pl.multiple_of(block * 256 + 128 * i, 128), 128)] for i in range(2)], axis=1)
            q_ids = q_ids.astype(F32)
            biases = []
            for place in range(tiles):
                tile = picked[place]
                if first:
                    got = g_ref[half, tile, pl.ds(block * 512 + sub, 256, stride=2), :].T
                else:
                    rows = pl.ds(tile * 256 + sub, 128, stride=2)
                    got = jnp.concatenate([g_ref[half, block * 2, rows, :], g_ref[half, block * 2 + 1, rows, :]], axis=1)
                k_ids = ids_buf[tile]
                same = jnp.concatenate([k_ids, k_ids], axis=1) == q_ids
                biases.append((got + jnp.where(same, add, 0.0)) * LOG2E)
            for line in range(4):
                q = q_buf[line, :, q_at]
                scores = []
                for place in range(tiles):
                    k_at = pl.ds(pl.multiple_of(picked[place] * 128, 128), 128)
                    keys = k_buf[line, k_at, :] * head_mask
                    scores.append(dot(keys, q) * scale + biases[place])
                peak = functools.reduce(jnp.maximum, [jnp.max(s, axis=0, keepdims=True) for s in scores])
                weights = [jnp.exp2(s - peak) for s in scores]
                total = functools.reduce(jnp.add, [jnp.sum(w, axis=0, keepdims=True) for w in weights])
                mixed = None
                for place in range(tiles):
                    k_at = pl.ds(pl.multiple_of(picked[place] * 128, 128), 128)
                    term = dot(v_buf[line, head_at, k_at], weights[place].astype(BF16))
                    mixed = term if mixed is None else mixed + term
                gated = mixed * (1.0 / total) * gate_buf[line, head_at, q_at]
                mix_buf[line, head_at, q_at] = gated.astype(BF16)
            return carry

        lax.fori_loop(0, 8, body, 0)

    for tiles in range(1, 5):
        pl.when(count == tiles)(functools.partial(run, tiles))

    w_o = output_ref[...]
    for line in range(4):
        emit(line, lines(line) + dot(mix_buf[line], w_o, 0, 0))


ATTENTION_SCRATCH = [
    pltpu.VMEM((4, 512, 128), BF16),
    pltpu.VMEM((4, 128, 512), BF16),
    pltpu.VMEM((4, 128, 512), BF16),
    pltpu.VMEM((4, 128, 512), F32),
    pltpu.VMEM((4, 128, 512), BF16),
    pltpu.VMEM((4, 128, 128), F32),
]


def row_kernel(
    mask_ref, add_ref, x_ref, g_ref, ids_ref, project_ref, output_ref, bias_w_ref, pair_ref, blk_ref, line_buf, send_buf, *scratch
):
    row, _, _ = my_place()
    flags = [mask_ref[row // 4, tile] for tile in range(4)]

    def lines(line):
        return x_ref[line].astype(F32)

    def emit(line, value):
        value = value.astype(BF16).astype(F32)
        write_bias_block(blk_ref, line, dot(bias_w_ref[...], layer_norm(value).astype(BF16), 0, 1))
        line_buf[...] = value
        for j in range(4):
            send_buf[pl.ds(line * 4 + j, 128, stride=16), :] = line_buf[pl.ds(j, 128, stride=4), :]

    attention(
        True, lines, flags, g_ref, ids_ref, lambda head: add_ref[0, head], project_ref, output_ref, emit, *scratch
    )
    pair_ref[...] = send_buf[...].reshape(128, 16, 128).astype(BF16)


def row_attention(mask, add, x, g, ids, project, output, bias_w):
    return pl.pallas_call(
        row_kernel,
        out_shape=(jax.ShapeDtypeStruct((128, 16, 128), BF16), jax.ShapeDtypeStruct((2, 4, 8, 128), F32)),
        in_specs=[smem(), smem()] + [vmem()] * 6,
        out_specs=(vmem(), vmem()),
        scratch_shapes=[pltpu.VMEM((512, 128), F32), pltpu.VMEM((2048, 128), F32)] + ATTENTION_SCRATCH,
        compiler_params=pltpu.CompilerParams(vmem_limit_bytes=VMEM_LIMIT),
        name="row_attention",
    )(mask, add, x, g, ids, project, output, bias_w)


def col_kernel(
    mask_ref,
    add_ref,
    cols_ref,
    g_ref,
    ids_ref,
    project_ref,
    output_ref,
    left_ref,
    right_ref,
    edge_ref,
    second_ref,
    cols_buf,
    edge_buf,
    *scratch,
):
    row, _, _ = my_place()
    flags = [mask_ref[tile, row // 4] for tile in range(4)]
    cols_buf[...] = cols_ref[...].astype(F32).reshape(2048, 128)

    def lines(line):
        return cols_buf[pl.ds(line, 512, stride=4), :]

    def emit(line, value):
        rounded = value.astype(BF16)
        second_ref[:, line * 32 : (line + 1) * 32, :] = rounded.reshape(16, 32, 128)
        normed = layer_norm(rounded.astype(F32)).astype(BF16)
        for side, w_ref in enumerate((left_ref, right_ref)):
            both = dot(w_ref[...], normed, 0, 1)
            act = sigmoid(both[128:]) * both[:128]
            for tile in range(4):
                edge_buf[pl.ds(line * 8 + side * 4 + tile, 128, stride=32), :] = act[
                    :, tile * 128 : (tile + 1) * 128
                ] * flags[tile].astype(F32)

    attention(
        False, lines, flags, g_ref, ids_ref, lambda head: add_ref[1, head], project_ref, output_ref, emit, *scratch
    )
    edge_ref[...] = edge_buf[...].reshape(128, 32, 128).astype(BF16)


def col_attention(mask, add, cols, g, ids, project, output, left, right):
    return pl.pallas_call(
        col_kernel,
        out_shape=(jax.ShapeDtypeStruct((128, 32, 128), BF16), jax.ShapeDtypeStruct((16, 128, 128), BF16)),
        in_specs=[smem(), smem()] + [vmem()] * 7,
        out_specs=(vmem(), vmem()),
        scratch_shapes=[pltpu.VMEM((2048, 128), F32), pltpu.VMEM((4096, 128), F32)] + ATTENTION_SCRATCH,
        compiler_params=pltpu.CompilerParams(vmem_limit_bytes=VMEM_LIMIT),
        name="col_attention",
    )(mask, add, cols, g, ids, project, output, left, right)


def triangle_kernel(
    edge_ref,
    second_ref,
    gate_w_ref,
    out_w_ref,
    out_ref,
    edge_in,
    second_in,
    edge_buf,
    prod_send,
    prod_in,
    x_buf,
    gate_buf,
    norm_buf,
    es,
    er,
    el,
    ss,
    sr,
    sl,
    ps,
    pr,
    pl_,
):
    row, col, dev = my_place()
    greet_all()
    edges = (edge_ref, edge_in, es, er, el)
    all_to_all_start(*edges)
    slot = lax.rem(dev, 16)
    grid_col = dev // 16

    def send_second(step, carry):
        to_row = lax.rem(row + step, 16)

        @pl.when(jnp.logical_and(to_row == row, grid_col == col))
        def _():
            pltpu.make_async_copy(second_ref.at[to_row], second_in.at[slot], sl).start()

        @pl.when(jnp.logical_not(jnp.logical_and(to_row == row, grid_col == col)))
        def _():
            pltpu.make_async_remote_copy(
                src_ref=second_ref.at[to_row],
                dst_ref=second_in.at[slot],
                send_sem=ss,
                recv_sem=sr,
                device_id=(to_row, grid_col),
                device_id_type=MESH,
            ).start()

        return carry

    lax.fori_loop(0, 16, send_second, 0)
    all_to_all_recv(*edges)
    edge_buf[...] = edge_in[...].astype(F32).reshape(4096, 128)
    right = jnp.concatenate([edge_buf[pl.ds(4 + tile, 512, stride=8), :] for tile in range(4)], axis=1).astype(BF16)
    low = lax.broadcasted_iota(jnp.int32, (16, 128), 1) < 64
    for tile in range(4):
        left = edge_buf[pl.ds(tile, 512, stride=8), :].astype(BF16)
        product = dot(left, right, 0, 0)
        for sub in range(4):
            for t in range(4):
                a = product[sub * 32 : sub * 32 + 16, t * 128 : (t + 1) * 128]
                b = product[sub * 32 + 16 : sub * 32 + 32, t * 128 : (t + 1) * 128]
                block = (tile * 4 + sub) * 8 + 2 * t
                prod_send[block] = jnp.where(low, a, pltpu.roll(b, 64, 1)).astype(BF16)
                prod_send[block + 1] = jnp.where(low, pltpu.roll(a, 64, 1), b).astype(BF16)
    products = (prod_send, prod_in, ps, pr, pl_)
    all_to_all_start(*products)

    own_sent = grid_col == col

    @pl.when(own_sent)
    def _():
        drain(second_in.at[0], sl)
        drain(second_in.at[pl.ds(0, 15)], sr)
        drain(second_ref.at[pl.ds(0, 15)], ss)

    @pl.when(jnp.logical_not(own_sent))
    def _():
        drain(second_in, sr)
        drain(second_ref, ss)

    gate_w = gate_w_ref[...]

    def gates(j, carry):
        at = pl.multiple_of(j * 128, 128)
        x = second_in[j].astype(F32)
        gate = sigmoid(dot(layer_norm(x).astype(BF16), gate_w))
        for sub in range(4):
            x_buf[pl.ds(j * 4 + sub, 32, stride=64), :] = x[sub * 32 : (sub + 1) * 32]
            gate_buf[pl.ds(j * 4 + sub, 32, stride=64), :] = gate[sub * 32 : (sub + 1) * 32]
        return carry

    lax.fori_loop(0, 16, gates, 0)
    all_to_all_recv(*products)
    product = prod_in[...].astype(F32)
    center = product - jnp.mean(product, axis=0, keepdims=True)
    spread = jnp.mean(center * center, axis=0, keepdims=True)
    norm_buf[...] = (center * lax.rsqrt(spread + 1e-05)).reshape(2048, 128)
    out_w = out_w_ref[...]
    for s in range(16):
        update = dot(norm_buf[pl.ds(s, 128, stride=16), :].astype(BF16), out_w, 0, 0)
        for half in range(2):
            i = half * 16 + s
            at = pl.ds(i * 64, 64)
            out_ref[i] = (x_buf[at, :] + gate_buf[at, :] * update[half * 64 : (half + 1) * 64]).astype(BF16)
    all_to_all_sent(*edges)
    all_to_all_sent(*products)


def triangle(edge, second, gate_w, out_w):
    return pl.pallas_call(
        triangle_kernel,
        out_shape=jax.ShapeDtypeStruct((32, 64, 128), BF16),
        in_specs=[vmem()] * 4,
        out_specs=vmem(),
        scratch_shapes=[
            pltpu.VMEM((128, 32, 128), BF16),
            pltpu.VMEM((16, 128, 128), BF16),
            pltpu.VMEM((4096, 128), F32),
            pltpu.VMEM((128, 16, 128), BF16),
            pltpu.VMEM((128, 16, 128), BF16),
            pltpu.VMEM((2048, 128), F32),
            pltpu.VMEM((2048, 128), F32),
            pltpu.VMEM((2048, 128), F32),
        ]
        + [pltpu.SemaphoreType.DMA] * 9,
        compiler_params=pltpu.CompilerParams(
            collective_id=2, has_side_effects=True, vmem_limit_bytes=VMEM_LIMIT
        ),
        name="triangle",
    )(edge, second, gate_w, out_w)


def shards(
    pair_rep,
    tile_mask,
    chain_ids,
    chain_bias,
    row_project,
    row_bias_proj,
    row_output,
    col_project,
    col_bias_proj,
    col_output,
    tri_left,
    tri_right,
    tri_gate,
    tri_output,
):
    ids = chain_ids.reshape(1, 512)
    g_rows = start(pair_rep, row_bias_proj)
    pair, blk = row_attention(
        tile_mask, chain_bias, pair_rep, g_rows, ids, row_project, row_output, col_bias_proj
    )
    g_cols, cols = middle(blk, pair)
    edge, second = col_attention(
        tile_mask, chain_bias, cols, g_cols, ids, col_project, col_output, tri_left, tri_right
    )
    return triangle(edge, second, tri_gate, tri_output)


def solution(mesh):
    spec = P(("row", "col"), None, None)
    return jax.shard_map(
        shards,
        mesh=mesh,
        in_specs=(spec,) + (P(),) * 13,
        out_specs=P("row", "col", None),
        check_vma=False,
    )
```

time: 920 us -> 146 us (0.16)
  waiting for transfers between devices: 323 us -> 0 us
  local copies, waits for them, and re-layouts: 243 us -> 3.55 us
  matrix products: 157 us -> 0 us
  Pallas kernels: 0 us -> 142 us
  loops' own time: 84.4 us -> 0 us
  other arithmetic: 63 us -> 0 us
  starting transfers between devices: 28.3 us -> 0 us
  between operations: 13.8 us -> 0.16 us
    all_to_all x5 -> x0, waiting for transfers between devices: 224 us -> none  [the longest x4 211 us: one_round(): lax.all_to_all(outgoing, ('row', 'col'), split_axis=0, concat_axis=0, til...]
    dot_general x81 -> x0, matrix products: 157 us -> none  [the longest x32 73.4 us: one_block(): jnp.einsum('hqk,khd->qhd', attention, value_line, preferred_element_type=...]
    pallas_call x0 -> x5, Pallas kernels: none -> 142 us  [the longest x1 42 us: triangle(): pl.pallas_call(triangle_kernel, out_shape=jax.ShapeDtypeStruct((32, 64, 1...]
    dynamic_slice x156 -> x0, local copies, waits for them, and re-layouts: 109 us -> none  [the longest x32 61.2 us: one_block(): lax.dynamic_slice_in_dim(bias_all, offset, query_rows, 2).transpose(0, 2, 1)]
    all_gather x2 -> x0, waiting for transfers between devices: 98.9 us -> none  [the longest x1 67.3 us: shards(): bias_all = lax.all_gather(bias_rows, ('row', 'col'), axis=1, tiled=True)]
    another operation x3 -> x0, loops' own time: 84.4 us -> none  [the longest x2 83.8 us: attend_lines(): lax.map(one_block, jnp.arange(line_count * per_line, dtype=jnp.int32))]
    slice x13 -> x0, local copies, waits for them, and re-layouts: 45.2 us -> none  [the longest x4 26.7 us: one_round(): received[:, block_rows:2 * block_rows]]
    convert_element_type x68 -> x0, other arithmetic: 39.4 us -> none  [the longest x32 32.6 us: one_block(): return (mixed_rows * jax.nn.sigmoid(gate_block)).astype(jnp.bfloat16)]
  transfers between devices with their start and end apart: 7 -> 0, of which waited for: 7 -> 0; matrix products, arithmetic and copies ran while one was open for 2% -> 0% of each run, Pallas kernels for 0% -> 0%
where the time goes in v1:
time: 146 us; the launch traced here: 145 us
  Pallas kernels  142 us (97%)
  local copies, waits for them, and re-layouts  3.55 us (2%)
    pallas_call x1, Pallas kernels, triangle(): pl.pallas_call(triangle_kernel, out_shape=jax.ShapeDtypeStruct((32, 64, 1...  42 us
    pallas_call x1, Pallas kernels, middle(): pl.pallas_call(middle_kernel, out_shape=(jax.ShapeDtypeStruct(G_SHAPE, F3...  39.9 us
    pallas_call x1, Pallas kernels, start(): pl.pallas_call(start_kernel, out_shape=jax.ShapeDtypeStruct(G_SHAPE, F32)...  32.5 us
    pallas_call x1, Pallas kernels, col_attention(): pl.pallas_call(col_kernel, out_shape=(jax.ShapeDtypeStruct((128, 32, 128)...  14.6 us
    pallas_call x1, Pallas kernels, row_attention(): pl.pallas_call(row_kernel, out_shape=(jax.ShapeDtypeStruct((128, 16, 128)...  12.8 us
    unnamed x27, local copies, waits for them, and re-layouts  3.55 us

profile of v1, /device:TPU:1, one launch (start us, length us, event | category | flops | bytes accessed | tf_op | source)
XLA Modules:
  0.0 145.5 jit_solution(7044903536837212363)
XLA Ops:
  0.0 0.0 copy-start.11
  0.0 0.0 copy-start.9
  0.0 0.0 copy-start.5
  0.0 0.0 copy-start.10
  0.0 0.9 copy.15.bias_w_ref
  0.9 0.8 copy.16.bias_w_ref
  1.7 0.0 copy-start
  1.7 1.0 copy-done
  2.7 0.0 copy-start.1
  2.7 0.0 copy-start.2
  2.7 0.0 copy-start.3
  2.7 0.0 copy-start.4
  2.7 0.0 copy-start.6
  2.7 32.5 %bias_gather.1.g_ref = f32[2,4,1024,128]{3,2,1,0:T(8,128)} custom-call(bf16[4,512,128]{2,1,0:T(8,128)(2,1)S(1)} %copy-done, bf16[128,4]{1,0:T(8,128)(2,1)S(1)} %copy.15.bias_w_ref), custom_call_target="tpu_custom_call" | custom-call | tf_op jit(solution)/shard_map/bias_gather/pallas_call | solution.py:180
  35.3 0.0 copy-done.11
  35.3 0.0 copy-done.9
  35.3 0.0 copy-done.5
  35.3 0.0 copy-done.10
  35.3 0.0 copy-done.1
  35.3 0.0 copy-start.7
  35.3 0.0 copy-start.8
  35.3 12.8 %row_attention.1 = (bf16[128,16,128]{2,1,0:T(8,128)(2,1)S(1)}, f32[2,4,8,128]{3,2,1,0:T(8,128)S(1)}) custom-call(s32[4,4]{1,0:T(4,128)S(1)} %copy-done.9, f32[2,4]{1,0:T(2,128)S(1)} %copy-done.11, bf16[4,512,128]{2,1,0:T(8,128)(2,1)S(1)} %copy-done, f32[2,4,1024,128]{3,2,1,0:T(8,128)} %bias_gather.1.g_ref, s32[1,512]{1,0:T(1,128)S(1)} %bitcast.1, ...), custom_call_target="tpu_custom_call" | custom-call | tf_op jit(solution)/shard_map/row_attention/pallas_call | solution.py:372
  48.1 39.9 %columns_and_bias.1 = (f32[2,4,1024,128]{3,2,1,0:T(8,128)}, bf16[128,16,128]{2,1,0:T(8,128)(2,1)S(1)}) custom-call(f32[2,4,8,128]{3,2,1,0:T(8,128)S(1)} %get-tuple-element.11.blk_ref, bf16[128,16,128]{2,1,0:T(8,128)(2,1)S(1)} %get-tuple-element.12.pair_ref), custom_call_target="tpu_custom_call" | custom-call | tf_op jit(solution)/shard_map/columns_and_bias/pallas_call | solution.py:246
  88.0 0.0 copy-done.2
  88.0 0.0 copy-done.3
  88.0 0.0 copy-done.4
  88.0 0.0 copy-done.6
  88.0 14.6 %col_attention.1 = (bf16[128,32,128]{2,1,0:T(8,128)(2,1)S(1)}, bf16[16,128,128]{2,1,0:T(8,128)(2,1)S(1)}) custom-call(s32[4,4]{1,0:T(4,128)S(1)} %copy-done.9, f32[2,4]{1,0:T(2,128)S(1)} %copy-done.11, bf16[128,16,128]{2,1,0:T(8,128)(2,1)S(1)} %get-tuple-element.13.cols_ref, f32[2,4,1024,128]{3,2,1,0:T(8,128)} %get-tuple-element.14.g_ref, ...), custom_call_target="tpu_custom_call" | custom-call | tf_op jit(solution)/shard_map/col_attention/pallas_call | solution.py:425
  102.6 0.0 copy-done.7
  102.6 0.0 copy-done.8
  102.7 42.0 %triangle.1 = bf16[32,64,128]{2,1,0:T(8,128)(2,1)S(1)} custom-call(bf16[128,32,128]{2,1,0:T(8,128)(2,1)S(1)} %get-tuple-element.15.edge_ref, bf16[16,128,128]{2,1,0:T(8,128)(2,1)S(1)} %get-tuple-element.16.second_ref, bf16[128,128]{1,0:T(8,128)(2,1)S(1)} %copy-done.7, bf16[128,128]{1,0:T(8,128)(2,1)S(1)} %copy-done.8), custom_call_target="tpu_custom_call" | custom-call | tf_op jit(solution)/shard_map/triangle/pallas_call | solution.py:547
  144.7 0.8 copy.18
Async XLA Ops:
  0.0 35.3 %copy-start.11 = (f32[2,4]{1,0:T(2,128)S(1)}, f32[2,4]{1,0:T(2,128)}, u32[]{:S(2)}) copy-start(f32[2,4]{1,0:T(2,128)} %add_ref.3) | copy-start | bytes 100
  0.0 35.3 %copy-start.9 = (s32[4,4]{1,0:T(4,128)S(1)}, s32[4,4]{1,0:T(4,128)}, u32[]{:S(2)}) copy-start(s32[4,4]{1,0:T(4,128)} %mask_ref.3) | copy-start | bytes 196
  0.0 35.3 %copy-start.5 = (bf16[128,128]{1,0:T(8,128)(2,1)S(1)}, bf16[128,128]{1,0:T(8,128)(2,1)}, u32[]{:S(2)}) copy-start(bf16[128,128]{1,0:T(8,128)(2,1)} %output_ref.2) | copy-start | bytes 98308
  0.0 35.3 %copy-start.10 = (s32[512]{0:T(512)S(1)}, s32[512]{0:T(512)}, u32[]{:S(2)}) copy-start(s32[512]{0:T(512)} %param.16) | copy-start | bytes 6148
  1.7 1.0 copy-start
  2.7 32.6 %copy-start.1 = (bf16[128,512]{1,0:T(8,128)(2,1)S(1)}, bf16[128,512]{1,0:T(8,128)(2,1)}, u32[]{:S(2)}) copy-start(bf16[128,512]{1,0:T(8,128)(2,1)} %project_ref.2) | copy-start | bytes 393220
  2.7 85.3 %copy-start.2 = (bf16[128,512]{1,0:T(8,128)(2,1)S(1)}, bf16[128,512]{1,0:T(8,128)(2,1)}, u32[]{:S(2)}) copy-start(bf16[128,512]{1,0:T(8,128)(2,1)} %project_ref.3) | copy-start | bytes 393220
  2.7 85.3 %copy-start.3 = (bf16[128,256]{1,0:T(8,128)(2,1)S(1)}, bf16[128,256]{1,0:T(8,128)(2,1)}, u32[]{:S(2)}) copy-start(bf16[128,256]{1,0:T(8,128)(2,1)} %left_ref.1) | copy-start | bytes 196612
  2.7 85.3 %copy-start.4 = (bf16[128,256]{1,0:T(8,128)(2,1)S(1)}, bf16[128,256]{1,0:T(8,128)(2,1)}, u32[]{:S(2)}) copy-start(bf16[128,256]{1,0:T(8,128)(2,1)} %right_ref.1) | copy-start | bytes 196612
  2.7 85.3 %copy-start.6 = (bf16[128,128]{1,0:T(8,128)(2,1)S(1)}, bf16[128,128]{1,0:T(8,128)(2,1)}, u32[]{:S(2)}) copy-start(bf16[128,128]{1,0:T(8,128)(2,1)} %output_ref.3) | copy-start | bytes 98308
  35.3 67.3 %copy-start.7 = (bf16[128,128]{1,0:T(8,128)(2,1)S(1)}, bf16[128,128]{1,0:T(8,128)(2,1)}, u32[]{:S(2)}) copy-start(bf16[128,128]{1,0:T(8,128)(2,1)} %gate_w_ref.1) | copy-start | bytes 98308
  35.3 67.3 %copy-start.8 = (bf16[128,128]{1,0:T(8,128)(2,1)S(1)}, bf16[128,128]{1,0:T(8,128)(2,1)}, u32[]{:S(2)}) copy-start(bf16[128,128]{1,0:T(8,128)(2,1)} %out_w_ref.1) | copy-start | bytes 98308

commit v2 on v1

v2 whole, which is shorter than its diff:
```python
import functools
import math

import jax
import jax.numpy as jnp
from jax import lax
from jax.experimental import pallas as pl
from jax.experimental.pallas import tpu as pltpu
from jax.sharding import PartitionSpec as P

MESH = pl.DeviceIdType.MESH
F32 = jnp.float32
BF16 = jnp.bfloat16
DEVS = 128
LOG2E = 1.4426950408889634
VMEM_LIMIT = 50 * 2**20


def vmem():
    return pl.BlockSpec(memory_space=pltpu.VMEM)


def smem():
    return pl.BlockSpec(memory_space=pltpu.SMEM)


def layer_norm(values):
    center = values - jnp.mean(values, axis=-1, keepdims=True)
    spread = jnp.mean(center * center, axis=-1, keepdims=True)
    return center * lax.rsqrt(spread + 1e-05)


def dot(a, b, ca=1, cb=0):
    return lax.dot_general(a, b, (((ca,), (cb,)), ((), ())), preferred_element_type=F32)


def sigmoid(x):
    return 1.0 / (1.0 + jnp.exp(-x))


def my_place():
    row, col = lax.axis_index("row"), lax.axis_index("col")
    return row, col, row * 8 + col


def drain(ref, sem):
    pltpu.make_async_copy(ref, ref, sem).wait()


def bias_step(w_ref):
    w = w_ref[...].astype(F32)
    length = jnp.sqrt(jnp.sum(w * w, axis=1, keepdims=True))
    return jnp.maximum(length, 1e-20) * (11.4 / 32766.0)


def code_bias(blk32, line, w_ref, inverse, normed):
    coded = jnp.round(dot(w_ref[...], normed, 1, 1) * inverse).astype(jnp.int32)
    for tile in range(4):
        blk32[tile // 2, tile % 2, line * 4 : line * 4 + 4, :] = coded[:, tile * 128 : (tile + 1) * 128]


def signal_partners():
    row, col, _ = my_place()
    core, z, y, x = col % 2, col // 2, row % 4, row // 4
    partners = []
    for step in range(4):
        for flip in range(2):
            if step or flip:
                partners.append((row, lax.rem(z + step, 4) * 2 + lax.rem(core + flip, 2)))
    for step in (1, 2, 3):
        partners.append((x * 4 + lax.rem(y + step, 4), col))
        partners.append((lax.rem(x + step, 4) * 4 + y, col))
    barrier = pltpu.get_barrier_semaphore()
    for partner in partners:
        pl.semaphore_signal(barrier, inc=1, device_id=partner, device_id_type=MESH)
    return len(partners)


def signal_all():
    _, _, dev = my_place()
    barrier = pltpu.get_barrier_semaphore()

    def step(off, carry):
        dest = lax.rem(dev + off, DEVS)
        pl.semaphore_signal(barrier, inc=1, device_id=(dest // 8, dest % 8), device_id_type=MESH)
        return carry

    lax.fori_loop(1, DEVS, step, 0)
    return DEVS - 1


def await_signals(count):
    pl.semaphore_wait(pltpu.get_barrier_semaphore(), count)


G_SHAPE = (2, 128, 2, 16, 128)
GATHER_SEMS = [pltpu.SemaphoreType.DMA((n,)) for n in (1, 8, 8, 4, 4, 16, 16, 16, 16)]
FORWARD = False


def gather_bias(blk_ref, g_ref, own_sem, zs, zr, as_, ar_, bs, br, fs, fr, work=()):
    row, col, dev = my_place()
    core, z, y, x = col % 2, col // 2, row % 4, row // 4
    a_me = jnp.where(core == 0, y, x)
    b_me = jnp.where(core == 0, x, y)
    sibling = (row, z * 2 + 1 - core)
    work = list(work)

    def do_work():
        if work:
            work.pop(0)()

    def row_of(a, b):
        a, b = lax.rem(a, 4), lax.rem(b, 4)
        return jnp.where(core == 0, b * 4 + a, a * 4 + b)

    def part(half, start, size):
        return g_ref.at[half, pl.ds(start, size)]

    started = []

    def send(src, dst, ssem, rsem, device):
        copy = pltpu.make_async_remote_copy(
            src_ref=src, dst_ref=dst, send_sem=ssem, recv_sem=rsem, device_id=device, device_id_type=MESH
        )
        copy.start()
        started.append(copy)

    near = [(1, 0), (3, 0), (0, 1), (1, 1), (3, 1), (2, 0), (2, 1)]
    for step, flip in near:
        to_core = lax.rem(core + flip, 2)
        send(
            blk_ref.at[pl.ds(to_core, 1)],
            g_ref.at[pl.ds(to_core, 1), dev],
            zs.at[step * 2 + flip],
            zr.at[(4 - step) % 4 * 2 + flip],
            (row, lax.rem(z + step, 4) * 2 + to_core),
        )
    own = pltpu.make_async_copy(blk_ref.at[pl.ds(core, 1)], g_ref.at[pl.ds(core, 1), dev], own_sem.at[0])
    own.start()
    do_work()
    own.wait()
    for step, flip in near:
        source = row * 8 + lax.rem(z + step, 4) * 2 + lax.rem(core + flip, 2)
        drain(g_ref.at[pl.ds(core, 1), source], zr.at[step * 2 + flip])

    def block(da, db):
        return part(core, row_of(a_me + da, b_me + db) * 8, 8)

    def to_sibling(da, db):
        ref = block(da, db)
        send(ref, ref, fs.at[da * 4 + db], fr.at[da * 4 + db], sibling)

    def along_b(da, db, step):
        ref = block(da, db)
        rel = (db - step) % 4
        send(ref, ref, bs.at[da * 4 + rel], br.at[da * 4 + rel], (row_of(a_me, b_me + step), col))

    def spread(da):
        along_b(da, 0, 1)
        along_b(da, 0, 3)
        if not FORWARD:
            along_b(da, 0, 2)
        to_sibling(da, 0)

    for step in (1, 3, 2):
        ref = block(0, 0)
        send(ref, ref, as_.at[step], ar_.at[4 - step], (row_of(a_me + step, b_me), col))
    spread(0)
    do_work()
    for da in (1, 3, 2):
        drain(block(da, 0), ar_.at[da])
        spread(da)
    do_work()
    for da in (0, 1, 3, 2):
        for db in (3, 1):
            drain(block(da, db), br.at[da * 4 + db])
            if FORWARD and (db == 3) == (da in (0, 3)):
                along_b(da, db, 1 if db == 3 else 3)
            to_sibling(da, db)
    do_work()
    for da in (0, 1, 3, 2):
        drain(block(da, 2), br.at[da * 4 + 2])
        to_sibling(da, 2)
    while work:
        do_work()
    for db in (0, 3, 1, 2):
        for da in (0, 1, 3, 2):
            s_row = jnp.where(
                core == 1,
                lax.rem(x + db, 4) * 4 + lax.rem(y + da, 4),
                lax.rem(x + da, 4) * 4 + lax.rem(y + db, 4),
            )
            drain(part(1 - core, s_row * 8, 8), fr.at[da * 4 + db])
    for copy in started:
        copy.wait_send()


PROJECTED = (
    jax.ShapeDtypeStruct((4, 512, 128), BF16),
    jax.ShapeDtypeStruct((4, 128, 512), BF16),
    jax.ShapeDtypeStruct((4, 128, 512), BF16),
    jax.ShapeDtypeStruct((4, 128, 512), F32),
)


def project_line(line, normed, project_ref, k_ref, q_ref, v_ref, gate_ref):
    k_ref[line] = dot(normed, project_ref[:, 128:256]).astype(BF16)
    q_ref[line] = dot(project_ref[:, 0:128], normed, 0, 1).astype(BF16)
    both = dot(project_ref[:, 256:512], normed, 0, 1)
    v_ref[line] = both[:128].astype(BF16)
    gate_ref[line] = sigmoid(both[128:])


def start_kernel(x_ref, bias_w_ref, project_ref, g_ref, k_ref, q_ref, v_ref, gate_ref, blk32, blk, normed_buf, *sems):
    signals = signal_partners()
    inverse = 1.0 / bias_step(bias_w_ref)
    for line in range(4):
        normed = layer_norm(x_ref[line].astype(F32)).astype(BF16)
        normed_buf[line] = normed
        code_bias(blk32, line, bias_w_ref, inverse, normed)
    blk[...] = blk32[...].astype(jnp.int16)
    await_signals(signals)

    def work(line):
        project_line(line, normed_buf[line], project_ref, k_ref, q_ref, v_ref, gate_ref)

    gather_bias(blk, g_ref, *sems, work=[functools.partial(work, line) for line in range(4)])


BLK = [pltpu.VMEM((2, 2, 16, 128), jnp.int32), pltpu.VMEM((2, 2, 16, 128), jnp.int16)]


def start(x, bias_w, project):
    return pl.pallas_call(
        start_kernel,
        out_shape=(jax.ShapeDtypeStruct(G_SHAPE, jnp.int16),) + PROJECTED,
        in_specs=[vmem()] * 3,
        out_specs=(vmem(),) * 5,
        scratch_shapes=BLK + [pltpu.VMEM((4, 512, 128), BF16)] + GATHER_SEMS,
        compiler_params=pltpu.CompilerParams(
            collective_id=0, has_side_effects=True, vmem_limit_bytes=VMEM_LIMIT
        ),
        name="bias_gather",
    )(x, bias_w, project)


def all_to_all_some(src_ref, dst_ref, ssem, rsem, lsem, first, last):
    row, col, dev = my_place()

    def step(off, carry):
        dest = lax.rem(dev + off, DEVS)
        pltpu.make_async_remote_copy(
            src_ref=src_ref.at[dest],
            dst_ref=dst_ref.at[dev],
            send_sem=ssem,
            recv_sem=rsem,
            device_id=(dest // 8, dest % 8),
            device_id_type=MESH,
        ).start()
        return carry

    if first == 1:
        pltpu.make_async_copy(src_ref.at[dev], dst_ref.at[dev], lsem).start()
    lax.fori_loop(first, last, step, 0)


def all_to_all_start(*args):
    all_to_all_some(*args, 1, DEVS)


def all_to_all_recv(src_ref, dst_ref, ssem, rsem, lsem):
    drain(dst_ref.at[0], lsem)
    drain(dst_ref.at[pl.ds(0, DEVS - 1)], rsem)


def all_to_all_sent(src_ref, dst_ref, ssem, rsem, lsem):
    drain(src_ref.at[pl.ds(0, DEVS - 1)], ssem)


def middle_kernel(
    x_ref,
    mix_ref,
    output_ref,
    bias_w_ref,
    project_ref,
    g_ref,
    k_ref,
    q_ref,
    v_ref,
    gate_ref,
    cols_ref,
    line_buf,
    send_buf,
    tiles,
    cols_buf,
    blk32,
    blk,
    s0,
    s1,
    s2,
    *sems,
):
    signals = signal_all()
    inverse = 1.0 / bias_step(bias_w_ref)
    w_o = output_ref[...]
    for line in range(4):
        value = x_ref[line].astype(F32) + dot(mix_ref[line], w_o, 0, 0)
        value = value.astype(BF16).astype(F32)
        code_bias(blk32, line, bias_w_ref, inverse, layer_norm(value).astype(BF16))
        line_buf[line] = value
        for j in range(4):
            send_buf[pl.ds(line * 4 + j, 128, stride=16), :] = line_buf[line, pl.ds(j, 128, stride=4), :]
    blk[...] = blk32[...].astype(jnp.int16)
    tiles[...] = send_buf[...].reshape(128, 16, 128).astype(BF16)
    await_signals(signals)
    args = (tiles, cols_ref, s0, s1, s2)

    def project_all():
        all_to_all_recv(*args)
        cols_buf[...] = cols_ref[...].astype(F32).reshape(2048, 128)
        for line in range(4):
            normed = layer_norm(cols_buf[pl.ds(line, 512, stride=4), :]).astype(BF16)
            project_line(line, normed, project_ref, k_ref, q_ref, v_ref, gate_ref)

    work = [functools.partial(all_to_all_some, *args, lo, hi) for lo, hi in ((1, 33), (33, 81), (81, 128))]
    gather_bias(blk, g_ref, *sems, work=work + [project_all])
    all_to_all_sent(*args)


def middle(x, mix, output, bias_w, project):
    return pl.pallas_call(
        middle_kernel,
        out_shape=(jax.ShapeDtypeStruct(G_SHAPE, jnp.int16),)
        + PROJECTED
        + (jax.ShapeDtypeStruct((128, 16, 128), BF16),),
        in_specs=[vmem()] * 5,
        out_specs=(vmem(),) * 6,
        scratch_shapes=[
            pltpu.VMEM((4, 512, 128), F32),
            pltpu.VMEM((2048, 128), F32),
            pltpu.VMEM((128, 16, 128), BF16),
            pltpu.VMEM((2048, 128), F32),
        ]
        + BLK
        + [pltpu.SemaphoreType.DMA] * 3
        + GATHER_SEMS,
        compiler_params=pltpu.CompilerParams(
            collective_id=1, has_side_effects=True, vmem_limit_bytes=VMEM_LIMIT
        ),
        name="columns_and_bias",
    )(x, mix, output, bias_w, project)


def compact(flags):
    count = jnp.int32(0)
    picked = [jnp.int32(0)] * 4
    for tile in range(4):
        for place in range(4):
            hit = jnp.logical_and(flags[tile] > 0, count == place)
            picked[place] = jnp.where(hit, tile, picked[place])
        count = count + flags[tile]
    return picked, count


def attention_kernel(
    which, mask_ref, add_ref, g_ref, ids_ref, bias_w_ref, k_ref, q_ref, v_ref, gate_ref, mix_ref, bias_buf, code_buf, ids_buf
):
    row, _, _ = my_place()
    flags = [mask_ref[row // 4, t] if which == 0 else mask_ref[t, row // 4] for t in range(4)]
    scale = LOG2E * 32 ** (-0.5)
    ids = ids_ref[...].astype(F32)
    for tile in range(4):
        ids_buf[tile] = jnp.broadcast_to(ids[:, tile * 128 : (tile + 1) * 128], (128, 128)).T
    picked, count = compact(flags)
    steps = bias_step(bias_w_ref) * LOG2E
    adds = [add_ref[which, head] * LOG2E for head in range(4)]
    lanes = lax.broadcasted_iota(jnp.int32, (1, 128), 1) // 32
    head_masks = [jnp.where(lanes == head, 1.0, 0.0).astype(BF16) for head in range(4)]
    upper = lax.broadcasted_iota(jnp.int32, (64, 128), 0) < 32

    def run(tiles):
        def load_bias(place):
            tile = picked[place]
            if which == 0:
                code_buf[...] = g_ref[tile // 2, :, tile % 2].astype(F32).reshape(2048, 128)
            for q_tile in range(4):
                if which == 1:
                    got = g_ref[q_tile // 2, pl.ds(tile * 32, 32), q_tile % 2].astype(F32)
                    code_buf[0:512, :] = got.reshape(512, 128)
                same = ids_buf[tile] == ids[:, q_tile * 128 : (q_tile + 1) * 128]
                for head in range(4):
                    if which == 0:
                        code = code_buf[pl.ds(q_tile * 512 + head, 128, stride=4), :].T
                    else:
                        code = code_buf[pl.ds(head, 128, stride=4), :]
                    bias = code * steps[head : head + 1] + jnp.where(same, adds[head], 0.0)
                    bias_buf[head, place, :, q_tile * 128 : (q_tile + 1) * 128] = bias

        for place in range(tiles):
            load_bias(place)

        def body(step, carry):
            line, block = step // 2, step % 2
            q_at = pl.ds(pl.multiple_of(block * 256, 256), 256)
            q = q_ref[line, :, q_at]
            k_at = [pl.ds(pl.multiple_of(picked[place] * 128, 128), 128) for place in range(tiles)]
            scores = []
            for place in range(tiles):
                keys = k_ref[line, k_at[place], :]
                stacked = jnp.concatenate([keys * head_masks[head] for head in range(4)], axis=0)
                scores.append(dot(stacked, q))
            for pair in range(2):
                weights, totals = [], []
                for head in (2 * pair, 2 * pair + 1):
                    logits = [
                        scores[place][head * 128 : (head + 1) * 128] * scale + bias_buf[head, place, :, q_at]
                        for place in range(tiles)
                    ]
                    peak = functools.reduce(jnp.maximum, [jnp.max(s, axis=0, keepdims=True) for s in logits])
                    own = [jnp.exp2(s - peak) for s in logits]
                    totals.append(functools.reduce(jnp.add, [jnp.sum(w, axis=0, keepdims=True) for w in own]))
                    weights.append([w.astype(BF16) for w in own])
                rows = pl.ds(64 * pair, 64)
                mixed = None
                for place in range(tiles):
                    v = v_ref[line, rows, k_at[place]]
                    zero = jnp.zeros_like(v)
                    spread = jnp.concatenate([jnp.where(upper, v, zero), jnp.where(upper, zero, v)], axis=1)
                    term = dot(spread, jnp.concatenate([weights[0][place], weights[1][place]], axis=0))
                    mixed = term if mixed is None else mixed + term
                inverse = [1.0 / total for total in totals]
                for sub in range(2):
                    at = pl.ds(64 * pair + 32 * sub, 32)
                    gated = mixed[32 * sub : 32 * sub + 32] * inverse[sub] * gate_ref[line, at, q_at]
                    mix_ref[line, at, q_at] = gated.astype(BF16)
            return carry

        lax.fori_loop(0, 8, body, 0)

    for tiles in range(1, 5):
        pl.when(count == tiles)(functools.partial(run, tiles))


def attention(which, mask, add, g, ids, bias_w, projected):
    return pl.pallas_call(
        functools.partial(attention_kernel, which),
        out_shape=jax.ShapeDtypeStruct((4, 128, 512), BF16),
        in_specs=[smem(), smem()] + [vmem()] * 7,
        out_specs=vmem(),
        scratch_shapes=[
            pltpu.VMEM((4, 4, 128, 512), F32),
            pltpu.VMEM((2048, 128), F32),
            pltpu.VMEM((4, 128, 128), F32),
        ],
        compiler_params=pltpu.CompilerParams(vmem_limit_bytes=VMEM_LIMIT),
        name=("row_attention", "col_attention")[which],
    )(mask, add, g, ids, bias_w, *projected)


def triangle_kernel(
    mask_ref,
    cols_ref,
    mix_ref,
    output_ref,
    left_ref,
    right_ref,
    gate_w_ref,
    out_w_ref,
    out_ref,
    cols_buf,
    edge_ref,
    second_ref,
    edge_in,
    second_in,
    edge_buf,
    prod_send,
    prod_in,
    x_buf,
    gate_buf,
    norm_buf,
    es,
    er,
    el,
    ss,
    sr,
    sl,
    ps,
    pr,
    pl_,
):
    row, col, dev = my_place()
    signals = signal_all()
    flags = [mask_ref[tile, row // 4].astype(F32) for tile in range(4)]
    cols_buf[...] = cols_ref[...].astype(F32).reshape(2048, 128)
    w_o = output_ref[...]
    for line in range(4):
        value = cols_buf[pl.ds(line, 512, stride=4), :] + dot(mix_ref[line], w_o, 0, 0)
        rounded = value.astype(BF16)
        second_ref[:, line * 32 : (line + 1) * 32, :] = rounded.reshape(16, 32, 128)
        normed = layer_norm(rounded.astype(F32)).astype(BF16)
        for side, w_ref in enumerate((left_ref, right_ref)):
            both = dot(w_ref[...], normed, 0, 1)
            act = sigmoid(both[128:]) * both[:128]
            for tile in range(4):
                edge_buf[pl.ds(line * 8 + side * 4 + tile, 128, stride=32), :] = (
                    act[:, tile * 128 : (tile + 1) * 128] * flags[tile]
                )
    edge_ref[...] = edge_buf[...].reshape(128, 32, 128).astype(BF16)
    await_signals(signals)
    edges = (edge_ref, edge_in, es, er, el)
    all_to_all_start(*edges)
    slot = lax.rem(dev, 16)
    grid_col = dev // 16

    def send_second(step, carry):
        to_row = lax.rem(row + step, 16)

        @pl.when(jnp.logical_and(to_row == row, grid_col == col))
        def _():
            pltpu.make_async_copy(second_ref.at[to_row], second_in.at[slot], sl).start()

        @pl.when(jnp.logical_not(jnp.logical_and(to_row == row, grid_col == col)))
        def _():
            pltpu.make_async_remote_copy(
                src_ref=second_ref.at[to_row],
                dst_ref=second_in.at[slot],
                send_sem=ss,
                recv_sem=sr,
                device_id=(to_row, grid_col),
                device_id_type=MESH,
            ).start()

        return carry

    all_to_all_recv(*edges)
    lax.fori_loop(0, 16, send_second, 0)
    edge_buf[...] = edge_in[...].astype(F32).reshape(4096, 128)
    right = jnp.concatenate([edge_buf[pl.ds(4 + tile, 512, stride=8), :] for tile in range(4)], axis=1).astype(BF16)
    low = lax.broadcasted_iota(jnp.int32, (16, 128), 1) < 64
    for tile in range(4):
        left = edge_buf[pl.ds(tile, 512, stride=8), :].astype(BF16)
        product = dot(left, right, 0, 0)
        for sub in range(4):
            for t in range(4):
                a = product[sub * 32 : sub * 32 + 16, t * 128 : (t + 1) * 128]
                b = product[sub * 32 + 16 : sub * 32 + 32, t * 128 : (t + 1) * 128]
                block = (tile * 4 + sub) * 8 + 2 * t
                prod_send[block] = jnp.where(low, a, pltpu.roll(b, 64, 1)).astype(BF16)
                prod_send[block + 1] = jnp.where(low, pltpu.roll(a, 64, 1), b).astype(BF16)
    products = (prod_send, prod_in, ps, pr, pl_)
    all_to_all_start(*products)

    own_sent = grid_col == col

    @pl.when(own_sent)
    def _():
        drain(second_in.at[0], sl)
        drain(second_in.at[pl.ds(0, 15)], sr)
        drain(second_ref.at[pl.ds(0, 15)], ss)

    @pl.when(jnp.logical_not(own_sent))
    def _():
        drain(second_in, sr)
        drain(second_ref, ss)

    gate_w = gate_w_ref[...]

    def gates(j, carry):
        at = pl.multiple_of(j * 128, 128)
        x = second_in[j].astype(F32)
        gate = sigmoid(dot(layer_norm(x).astype(BF16), gate_w))
        for sub in range(4):
            x_buf[pl.ds(j * 4 + sub, 32, stride=64), :] = x[sub * 32 : (sub + 1) * 32]
            gate_buf[pl.ds(j * 4 + sub, 32, stride=64), :] = gate[sub * 32 : (sub + 1) * 32]
        return carry

    lax.fori_loop(0, 16, gates, 0)
    all_to_all_recv(*products)
    product = prod_in[...].astype(F32)
    center = product - jnp.mean(product, axis=0, keepdims=True)
    spread = jnp.mean(center * center, axis=0, keepdims=True)
    norm_buf[...] = (center * lax.rsqrt(spread + 1e-05)).reshape(2048, 128)
    out_w = out_w_ref[...]
    for s in range(16):
        update = dot(norm_buf[pl.ds(s, 128, stride=16), :].astype(BF16), out_w, 0, 0)
        for half in range(2):
            i = half * 16 + s
            at = pl.ds(i * 64, 64)
            out_ref[i] = (x_buf[at, :] + gate_buf[at, :] * update[half * 64 : (half + 1) * 64]).astype(BF16)
    all_to_all_sent(*edges)
    all_to_all_sent(*products)


def triangle(mask, cols, mix, output, left, right, gate_w, out_w):
    return pl.pallas_call(
        triangle_kernel,
        out_shape=jax.ShapeDtypeStruct((32, 64, 128), BF16),
        in_specs=[smem()] + [vmem()] * 7,
        out_specs=vmem(),
        scratch_shapes=[
            pltpu.VMEM((2048, 128), F32),
            pltpu.VMEM((128, 32, 128), BF16),
            pltpu.VMEM((16, 128, 128), BF16),
            pltpu.VMEM((128, 32, 128), BF16),
            pltpu.VMEM((16, 128, 128), BF16),
            pltpu.VMEM((4096, 128), F32),
            pltpu.VMEM((128, 16, 128), BF16),
            pltpu.VMEM((128, 16, 128), BF16),
            pltpu.VMEM((2048, 128), F32),
            pltpu.VMEM((2048, 128), F32),
            pltpu.VMEM((2048, 128), F32),
        ]
        + [pltpu.SemaphoreType.DMA] * 9,
        compiler_params=pltpu.CompilerParams(
            collective_id=2, has_side_effects=True, vmem_limit_bytes=VMEM_LIMIT
        ),
        name="triangle",
    )(mask, cols, mix, output, left, right, gate_w, out_w)


def shards(
    pair_rep,
    tile_mask,
    chain_ids,
    chain_bias,
    row_project,
    row_bias_proj,
    row_output,
    col_project,
    col_bias_proj,
    col_output,
    tri_left,
    tri_right,
    tri_gate,
    tri_output,
):
    ids = chain_ids.reshape(1, 512)
    row_w, col_w = row_bias_proj.T, col_bias_proj.T
    g_rows, *projected = start(pair_rep, row_w, row_project)
    mix = attention(0, tile_mask, chain_bias, g_rows, ids, row_w, projected)
    g_cols, *projected, cols = middle(pair_rep, mix, row_output, col_w, col_project)
    mix = attention(1, tile_mask, chain_bias, g_cols, ids, col_w, projected)
    return triangle(tile_mask, cols, mix, col_output, tri_left, tri_right, tri_gate, tri_output)


def solution(mesh):
    spec = P(("row", "col"), None, None)
    return jax.shard_map(
        shards,
        mesh=mesh,
        in_specs=(spec,) + (P(),) * 13,
        out_specs=P("row", "col", None),
        check_vma=False,
    )
```

time: 146 us -> 125 us (0.86)
  Pallas kernels: 142 us -> 118 us
  local copies, waits for them, and re-layouts: 3.55 us -> 6.71 us
    pallas_call x4, Pallas kernels: 99.7 us -> 68.4 us  [the longest x1 31.1 us: middle(): pl.pallas_call(middle_kernel, out_shape=(jax.ShapeDtypeStruct(G_SHAPE, jn...]
    pallas_call x1, Pallas kernels: 42 us -> 49.8 us  [triangle(): pl.pallas_call(triangle_kernel, out_shape=jax.ShapeDtypeStruct((32, 64, 1...]
    unnamed x27 -> x35, local copies, waits for them, and re-layouts: 3.55 us -> 6.71 us
where the time goes in v2:
time: 125 us
  Pallas kernels  118 us (94%)
  local copies, waits for them, and re-layouts  6.71 us (5%)
    pallas_call x1, Pallas kernels, triangle(): pl.pallas_call(triangle_kernel, out_shape=jax.ShapeDtypeStruct((32, 64, 1...  49.8 us
    pallas_call x1, Pallas kernels, middle(): pl.pallas_call(middle_kernel, out_shape=(jax.ShapeDtypeStruct(G_SHAPE, jn...  31.1 us
    pallas_call x1, Pallas kernels, start(): pl.pallas_call(start_kernel, out_shape=(jax.ShapeDtypeStruct(G_SHAPE, jnp...  25.8 us
    pallas_call x2, Pallas kernels, attention(): pl.pallas_call(functools.partial(attention_kernel, which), out_shape=jax....  11.5 us
    unnamed x35, local copies, waits for them, and re-layouts  6.71 us

profile of v2, /device:TPU:1, one launch (start us, length us, event | category | flops | bytes accessed | tf_op | source)
XLA Modules:
  0.0 125.1 jit_solution(9674410420021377751)
XLA Ops:
  0.0 0.0 copy-start
  0.0 1.0 copy-done
  1.0 0.0 copy-start.3
  1.0 0.9 copy-done.3
  1.9 0.0 copy-start.14
  1.9 0.7 copy-done.14
  2.6 25.8 %bias_gather.1 = (s16[2,128,2,16,128]{4,3,2,1,0:T(8,128)(2,1)}, bf16[4,512,128]{2,1,0:T(8,128)(2,1)S(1)}, bf16[4,128,512]{2,1,0:T(8,128)(2,1)S(1)}, bf16[4,128,512]{2,1,0:T(8,128)(2,1)S(1)}, f32[4,128,512]{2,1,0:T(8,128)S(1)}) custom-call(bf16[4,512,128]{2,1,0:T(8,128)(2,1)S(1)} %copy-done, bf16[4,128]{1,0:T(4,128)(2,1)S(1)} %bitcast.5, ...), custom_call_target="tpu_custom_call" | custom-call | tf_op jit(solution)/shard_map/bias_gather/pallas_call | solution.py:235
  28.5 0.0 copy-start.11
  28.5 0.7 copy-done.11
  29.1 0.0 copy-start.12
  29.1 0.7 copy-done.12
  29.8 0.0 copy-start.16
  29.8 0.7 copy-done.16
  30.5 0.0 copy-start.1
  30.5 0.0 copy-start.4
  30.5 0.0 copy-start.10
  30.5 0.0 copy-start.15
  30.5 0.0 copy-start.13
  30.5 5.7 %row_attention.1.mix_ref = bf16[4,128,512]{2,1,0:T(8,128)(2,1)S(1)} custom-call(s32[4,4]{1,0:T(4,128)S(1)} %copy-done.11, f32[2,4]{1,0:T(2,128)S(1)} %copy-done.16, s16[2,128,2,16,128]{4,3,2,1,0:T(8,128)(2,1)} %get-tuple-element.16.g_ref, s32[1,512]{1,0:T(1,128)S(1)} %bitcast.3, bf16[4,128]{1,0:T(4,128)(2,1)S(1)} %bitcast.6, ...), custom_call_target="tpu_custom_call" | custom-call | tf_op jit(solution)/shard_map/row_attention/pallas_call | solution.py:446
  36.3 0.0 copy-done.1
  36.3 0.0 copy-done.4
  36.3 0.0 copy-done.10
  36.3 0.0 copy-done.15
  36.3 31.1 %columns_and_bias.1 = (s16[2,128,2,16,128]{4,3,2,1,0:T(8,128)(2,1)}, bf16[4,512,128]{2,1,0:T(8,128)(2,1)S(1)}, bf16[4,128,512]{2,1,0:T(8,128)(2,1)S(1)}, bf16[4,...) custom-call(bf16[4,512,128]{2,1,0:T(8,128)(2,1)S(1)} %copy-done.1, ...), custom_call_target="tpu_custom_call" | custom-call | tf_op jit(solution)/shard_map/columns_and_bias/pallas_call | solution.py:332
  67.4 0.0 copy-done.13
  67.4 0.0 copy-start.2
  67.4 1.2 copy-done.2
  68.6 0.0 copy-start.5
  68.6 0.0 copy-start.6
  68.6 0.0 copy-start.7
  68.6 0.0 copy-start.8
  68.6 0.0 copy-start.9
  68.6 5.8 %col_attention.1.mix_ref = bf16[4,128,512]{2,1,0:T(8,128)(2,1)S(1)} custom-call(s32[4,4]{1,0:T(4,128)S(1)} %copy-done.11, f32[2,4]{1,0:T(2,128)S(1)} %copy-done.16, s16[2,128,2,16,128]{4,3,2,1,0:T(8,128)(2,1)} %get-tuple-element.22.g_ref, s32[1,512]{1,0:T(1,128)S(1)} %bitcast.4, bf16[4,128]{1,0:T(4,128)(2,1)S(1)} %bitcast.8, ...), custom_call_target="tpu_custom_call" | custom-call | tf_op jit(solution)/shard_map/col_attention/pallas_call | solution.py:446
  74.4 0.0 copy-done.5
  74.4 0.0 copy-done.6
  74.5 0.0 copy-done.7
  74.5 0.0 copy-done.8
  74.5 0.0 copy-done.9
  74.5 49.8 %triangle.1 = bf16[32,64,128]{2,1,0:T(8,128)(2,1)S(1)} custom-call(s32[4,4]{1,0:T(4,128)S(1)} %copy-done.11, bf16[128,16,128]{2,1,0:T(8,128)(2,1)S(1)} %get-tuple-element.21.cols_ref, bf16[4,128,512]{2,1,0:T(8,128)(2,1)S(1)} %col_attention.1.mix_ref, bf16[128,128]{1,0:T(8,128)(2,1)S(1)} %copy-done.7, bf16[128,256]{1,0:T(8,128)(2,1)S(1)} %copy-done.5, ...), custom_call_target="tpu_custom_call" | custom-call | tf_op jit(solution)/shard_map/triangle/pallas_call | solution.py:596
  124.3 0.8 copy.16
Async XLA Ops:
  0.0 1.0 copy-start
  1.0 0.9 copy-start.3
  1.9 0.7 copy-start.14
  28.5 0.7 copy-start.11
  29.1 0.7 copy-start.12
  29.8 0.7 copy-start.16
  30.5 5.8 %copy-start.1 = (bf16[4,512,128]{2,1,0:T(8,128)(2,1)S(1)}, bf16[4,512,128]{2,1,0:T(8,128)(2,1)}, u32[]{:S(2)}) copy-start(bf16[4,512,128]{2,1,0:T(8,128)(2,1)} %x_ref.3) | copy-start | bytes 1572868
  30.5 5.8 %copy-start.4 = (bf16[128,512]{1,0:T(8,128)(2,1)S(1)}, bf16[128,512]{1,0:T(8,128)(2,1)}, u32[]{:S(2)}) copy-start(bf16[128,512]{1,0:T(8,128)(2,1)} %project_ref.3) | copy-start | bytes 393220
  30.5 5.8 %copy-start.10 = (bf16[128,128]{1,0:T(8,128)(2,1)S(1)}, bf16[128,128]{1,0:T(8,128)(2,1)}, u32[]{:S(2)}) copy-start(bf16[128,128]{1,0:T(8,128)(2,1)} %output_ref.2) | copy-start | bytes 98308
  30.5 5.8 %copy-start.15 = (bf16[128,4]{0,1:T(4,128)(2,1)S(1)}, bf16[128,4]{0,1:T(4,128)(2,1)}, u32[]{:S(2)}) copy-start(bf16[128,4]{0,1:T(4,128)(2,1)} %param.22) | copy-start | bytes 3076
  30.5 36.8 %copy-start.13 = (s32[512]{0:T(512)S(1)}, s32[512]{0:T(512)}, u32[]{:S(2)}) copy-start(s32[512]{0:T(512)} %param.16) | copy-start | bytes 6148
  67.4 1.2 copy-start.2
  68.6 5.8 %copy-start.5 = (bf16[128,256]{1,0:T(8,128)(2,1)S(1)}, bf16[128,256]{1,0:T(8,128)(2,1)}, u32[]{:S(2)}) copy-start(bf16[128,256]{1,0:T(8,128)(2,1)} %left_ref.1) | copy-start | bytes 196612
  68.6 5.9 %copy-start.6 = (bf16[128,256]{1,0:T(8,128)(2,1)S(1)}, bf16[128,256]{1,0:T(8,128)(2,1)}, u32[]{:S(2)}) copy-start(bf16[128,256]{1,0:T(8,128)(2,1)} %right_ref.1) | copy-start | bytes 196612
  68.6 5.9 %copy-start.7 = (bf16[128,128]{1,0:T(8,128)(2,1)S(1)}, bf16[128,128]{1,0:T(8,128)(2,1)}, u32[]{:S(2)}) copy-start(bf16[128,128]{1,0:T(8,128)(2,1)} %output_ref.3) | copy-start | bytes 98308
  68.6 5.9 %copy-start.8 = (bf16[128,128]{1,0:T(8,128)(2,1)S(1)}, bf16[128,128]{1,0:T(8,128)(2,1)}, u32[]{:S(2)}) copy-start(bf16[128,128]{1,0:T(8,128)(2,1)} %gate_w_ref.1) | copy-start | bytes 98308
  68.6 5.9 %copy-start.9 = (bf16[128,128]{1,0:T(8,128)(2,1)S(1)}, bf16[128,128]{1,0:T(8,128)(2,1)}, u32[]{:S(2)}) copy-start(bf16[128,128]{1,0:T(8,128)(2,1)} %out_w_ref.1) | copy-start | bytes 98308

commit v3 on v2

--- a/solution.py
+++ b/solution.py
@@ -13,11 +13,15 @@
 BF16 = jnp.bfloat16
 DEVS = 128
 LOG2E = 1.4426950408889634
-VMEM_LIMIT = 50 * 2**20
+VMEM_LIMIT = 24 * 2**20
 
 
 def vmem():
     return pl.BlockSpec(memory_space=pltpu.VMEM)
+
+
+def hbm():
+    return pl.BlockSpec(memory_space=pltpu.HBM)
 
 
 def smem():
@@ -41,6 +45,14 @@
 def my_place():
     row, col = lax.axis_index("row"), lax.axis_index("col")
     return row, col, row * 8 + col
+
+
+def at_offset(offset):
+    row, col, _ = my_place()
+    x = lax.rem(row // 4 + offset // 32, 4)
+    y = lax.rem(row % 4 + offset // 8 % 4, 4)
+    z = lax.rem(col // 2 + offset // 2 % 4, 4)
+    return ((x * 4 + y) * 4 + z) * 2 + lax.rem(col % 2 + offset % 2, 2)
 
 
 def drain(ref, sem):
@@ -76,17 +88,30 @@
     return len(partners)
 
 
-def signal_all():
-    _, _, dev = my_place()
-    barrier = pltpu.get_barrier_semaphore()
-
-    def step(off, carry):
-        dest = lax.rem(dev + off, DEVS)
-        pl.semaphore_signal(barrier, inc=1, device_id=(dest // 8, dest % 8), device_id_type=MESH)
-        return carry
-
-    lax.fori_loop(1, DEVS, step, 0)
-    return DEVS - 1
+class Everyone:
+    def __init__(self, second, third):
+        self.second, self.third = second, third
+        self.count = signal_partners()
+
+    def next_round(self):
+        row, col, _ = my_place()
+        x, y = row // 4, row % 4
+        await_signals(self.count)
+        for step in (1, 2, 3):
+            for to in (x * 4 + lax.rem(y + step, 4), lax.rem(x + step, 4) * 4 + y):
+                pl.semaphore_signal(self.second, inc=1, device_id=(to, col), device_id_type=MESH)
+
+    def last_round(self):
+        row, col, _ = my_place()
+        pl.semaphore_wait(self.second, 6)
+        for step in range(1, 8):
+            pl.semaphore_signal(self.third, inc=1, device_id=(row, lax.rem(col + step, 8)), device_id_type=MESH)
+
+    def wait(self):
+        pl.semaphore_wait(self.third, 7)
+
+
+EVERYONE = [pltpu.SemaphoreType.REGULAR] * 2
 
 
 def await_signals(count):
@@ -212,44 +237,93 @@
     gate_ref[line] = sigmoid(both[128:])
 
 
-def start_kernel(x_ref, bias_w_ref, project_ref, g_ref, k_ref, q_ref, v_ref, gate_ref, blk32, blk, normed_buf, *sems):
+BLK = [pltpu.VMEM((2, 2, 16, 128), jnp.int32), pltpu.VMEM((2, 2, 16, 128), jnp.int16)]
+STEPS = jax.ShapeDtypeStruct((4, 128), F32)
+
+
+def start_kernel(
+    x_hbm,
+    bias_w_hbm,
+    project_hbm,
+    mask_hbm,
+    add_hbm,
+    ids_hbm,
+    g_ref,
+    k_ref,
+    q_ref,
+    v_ref,
+    gate_ref,
+    steps_ref,
+    mask_ref,
+    add_ref,
+    ids_ref,
+    x_buf,
+    bias_w_buf,
+    project_buf,
+    blk32,
+    blk,
+    normed_buf,
+    loaded,
+    *sems,
+):
+    loads = [pltpu.make_async_copy(bias_w_hbm, bias_w_buf, loaded.at[0])]
+    loads += [pltpu.make_async_copy(x_hbm.at[line], x_buf.at[line], loaded.at[1 + line]) for line in range(4)]
+    loads.append(pltpu.make_async_copy(project_hbm, project_buf, loaded.at[5]))
+    pairs = ((mask_hbm, mask_ref), (add_hbm, add_ref), (ids_hbm, ids_ref))
+    loads += [pltpu.make_async_copy(src, dst, loaded.at[6 + i]) for i, (src, dst) in enumerate(pairs)]
+    for load in loads:
+        load.start()
     signals = signal_partners()
-    inverse = 1.0 / bias_step(bias_w_ref)
+    loads[0].wait()
+    step = bias_step(bias_w_buf)
+    steps_ref[...] = jnp.broadcast_to(step, (4, 128))
+    inverse = 1.0 / step
     for line in range(4):
-        normed = layer_norm(x_ref[line].astype(F32)).astype(BF16)
+        loads[1 + line].wait()
+        normed = layer_norm(x_buf[line].astype(F32)).astype(BF16)
         normed_buf[line] = normed
-        code_bias(blk32, line, bias_w_ref, inverse, normed)
+        code_bias(blk32, line, bias_w_buf, inverse, normed)
     blk[...] = blk32[...].astype(jnp.int16)
     await_signals(signals)
 
     def work(line):
-        project_line(line, normed_buf[line], project_ref, k_ref, q_ref, v_ref, gate_ref)
+        if line == 0:
+            for load in loads[5:]:
+                load.wait()
+        project_line(line, normed_buf[line], project_buf, k_ref, q_ref, v_ref, gate_ref)
 
     gather_bias(blk, g_ref, *sems, work=[functools.partial(work, line) for line in range(4)])
 
 
-BLK = [pltpu.VMEM((2, 2, 16, 128), jnp.int32), pltpu.VMEM((2, 2, 16, 128), jnp.int16)]
-
-
-def start(x, bias_w, project):
+def start(x, bias_w, project, mask, add, ids):
     return pl.pallas_call(
         start_kernel,
-        out_shape=(jax.ShapeDtypeStruct(G_SHAPE, jnp.int16),) + PROJECTED,
-        in_specs=[vmem()] * 3,
-        out_specs=(vmem(),) * 5,
-        scratch_shapes=BLK + [pltpu.VMEM((4, 512, 128), BF16)] + GATHER_SEMS,
+        out_shape=(jax.ShapeDtypeStruct(G_SHAPE, jnp.int16),)
+        + PROJECTED
+        + (STEPS,)
+        + tuple(jax.ShapeDtypeStruct(a.shape, a.dtype) for a in (mask, add, ids)),
+        in_specs=[hbm()] * 6,
+        out_specs=(vmem(),) * 9,
+        scratch_shapes=[
+            pltpu.VMEM((4, 512, 128), BF16),
+            pltpu.VMEM((4, 128), BF16),
+            pltpu.VMEM((128, 512), BF16),
+        ]
+        + BLK
+        + [pltpu.VMEM((4, 512, 128), BF16), pltpu.SemaphoreType.DMA((9,))]
+        + GATHER_SEMS,
         compiler_params=pltpu.CompilerParams(
             collective_id=0, has_side_effects=True, vmem_limit_bytes=VMEM_LIMIT
         ),
         name="bias_gather",
-    )(x, bias_w, project)
+    )(x, bias_w, project, mask, add, ids)
 
 
 def all_to_all_some(src_ref, dst_ref, ssem, rsem, lsem, first, last):
     row, col, dev = my_place()
 
-    def step(off, carry):
-        dest = lax.rem(dev + off, DEVS)
+    def step(i, carry):
+        dest = at_offset(lax.rem(i * 37, DEVS))
         pltpu.make_async_remote_copy(
             src_ref=src_ref.at[dest],
             dst_ref=dst_ref.at[dev],
@@ -289,6 +363,7 @@
     q_ref,
     v_ref,
     gate_ref,
+    steps_ref,
     cols_ref,
     line_buf,
     send_buf,
@@ -296,13 +371,17 @@
     cols_buf,
     blk32,
     blk,
+    second_round,
+    third_round,
     s0,
     s1,
     s2,
     *sems,
 ):
-    signals = signal_all()
-    inverse = 1.0 / bias_step(bias_w_ref)
+    everyone = Everyone(second_round, third_round)
+    step = bias_step(bias_w_ref)
+    steps_ref[...] = jnp.broadcast_to(step, (4, 128))
+    inverse = 1.0 / step
     w_o = output_ref[...]
     for line in range(4):
         value = x_ref[line].astype(F32) + dot(mix_ref[line], w_o, 0, 0)
@@ -311,9 +390,13 @@
         line_buf[line] = value
         for j in range(4):
             send_buf[pl.ds(line * 4 + j, 128, stride=16), :] = line_buf[line, pl.ds(j, 128, stride=4), :]
+        if line == 1:
+            everyone.next_round()
+        if line == 3:
+            everyone.last_round()
     blk[...] = blk32[...].astype(jnp.int16)
     tiles[...] = send_buf[...].reshape(128, 16, 128).astype(BF16)
-    await_signals(signals)
+    everyone.wait()
     args = (tiles, cols_ref, s0, s1, s2)
 
     def project_all():
@@ -333,9 +416,9 @@
         middle_kernel,
         out_shape=(jax.ShapeDtypeStruct(G_SHAPE, jnp.int16),)
         + PROJECTED
-        + (jax.ShapeDtypeStruct((128, 16, 128), BF16),),
+        + (STEPS, jax.ShapeDtypeStruct((128, 16, 128), BF16)),
         in_specs=[vmem()] * 5,
-        out_specs=(vmem(),) * 6,
+        out_specs=(vmem(),) * 7,
         scratch_shapes=[
             pltpu.VMEM((4, 512, 128), F32),
             pltpu.VMEM((2048, 128), F32),
@@ -343,6 +426,7 @@
             pltpu.VMEM((2048, 128), F32),
         ]
         + BLK
+        + EVERYONE
         + [pltpu.SemaphoreType.DMA] * 3
         + GATHER_SEMS,
         compiler_params=pltpu.CompilerParams(
@@ -364,7 +448,7 @@
 
 
 def attention_kernel(
-    which, mask_ref, add_ref, g_ref, ids_ref, bias_w_ref, k_ref, q_ref, v_ref, gate_ref, mix_ref, bias_buf, code_buf, ids_buf
+    which, mask_ref, add_ref, g_ref, ids_ref, steps_ref, k_ref, q_ref, v_ref, gate_ref, mix_ref, bias_buf, code_buf, ids_buf
 ):
     row, _, _ = my_place()
     flags = [mask_ref[row // 4, t] if which == 0 else mask_ref[t, row // 4] for t in range(4)]
@@ -373,7 +457,7 @@
     for tile in range(4):
         ids_buf[tile] = jnp.broadcast_to(ids[:, tile * 128 : (tile + 1) * 128], (128, 128)).T
     picked, count = compact(flags)
-    steps = bias_step(bias_w_ref) * LOG2E
+    steps = steps_ref[...] * LOG2E
     adds = [add_ref[which, head] * LOG2E for head in range(4)]
     lanes = lax.broadcasted_iota(jnp.int32, (1, 128), 1) // 32
     head_masks = [jnp.where(lanes == head, 1.0, 0.0).astype(BF16) for head in range(4)]
@@ -442,7 +526,7 @@
         pl.when(count == tiles)(functools.partial(run, tiles))
 
 
-def attention(which, mask, add, g, ids, bias_w, projected):
+def attention(which, mask, add, g, ids, steps, projected):
     return pl.pallas_call(
         functools.partial(attention_kernel, which),
         out_shape=jax.ShapeDtypeStruct((4, 128, 512), BF16),
@@ -455,7 +539,7 @@
         ],
         compiler_params=pltpu.CompilerParams(vmem_limit_bytes=VMEM_LIMIT),
         name=("row_attention", "col_attention")[which],
-    )(mask, add, g, ids, bias_w, *projected)
+    )(mask, add, g, ids, steps, *projected)
 
 
 def triangle_kernel(
@@ -488,9 +572,11 @@
     ps,
     pr,
     pl_,
+    second_round,
+    third_round,
 ):
     row, col, dev = my_place()
-    signals = signal_all()
+    everyone = Everyone(second_round, third_round)
     flags = [mask_ref[tile, row // 4].astype(F32) for tile in range(4)]
     cols_buf[...] = cols_ref[...].astype(F32).reshape(2048, 128)
     w_o = output_ref[...]
@@ -506,8 +592,12 @@
                 edge_buf[pl.ds(line * 8 + side * 4 + tile, 128, stride=32), :] = (
                     act[:, tile * 128 : (tile + 1) * 128] * flags[tile]
                 )
+        if line == 1:
+            everyone.next_round()
+        if line == 3:
+            everyone.last_round()
     edge_ref[...] = edge_buf[...].reshape(128, 32, 128).astype(BF16)
-    await_signals(signals)
+    everyone.wait()
     edges = (edge_ref, edge_in, es, er, el)
     all_to_all_start(*edges)
     slot = lax.rem(dev, 16)
@@ -538,18 +628,37 @@
     edge_buf[...] = edge_in[...].astype(F32).reshape(4096, 128)
     right = jnp.concatenate([edge_buf[pl.ds(4 + tile, 512, stride=8), :] for tile in range(4)], axis=1).astype(BF16)
     low = lax.broadcasted_iota(jnp.int32, (16, 128), 1) < 64
-    for tile in range(4):
+    products = (prod_send, prod_in, ps, pr, pl_)
+
+    def send_product(slab, first):
+        def step(i, carry):
+            dest = at_offset(slab * 32 + lax.rem(i * 13, 32))
+            pltpu.make_async_remote_copy(
+                src_ref=prod_send.at[dest],
+                dst_ref=prod_in.at[dev],
+                send_sem=ps,
+                recv_sem=pr,
+                device_id=(dest // 8, dest % 8),
+                device_id_type=MESH,
+            ).start()
+            return carry
+
+        lax.fori_loop(first, 32, step, 0)
+
+    for slab in range(4):
+        tile = lax.rem(row // 4 + slab, 4)
         left = edge_buf[pl.ds(tile, 512, stride=8), :].astype(BF16)
         product = dot(left, right, 0, 0)
         for sub in range(4):
             for t in range(4):
                 a = product[sub * 32 : sub * 32 + 16, t * 128 : (t + 1) * 128]
                 b = product[sub * 32 + 16 : sub * 32 + 32, t * 128 : (t + 1) * 128]
-                block = (tile * 4 + sub) * 8 + 2 * t
+                block = tile * 32 + sub * 8 + 2 * t
                 prod_send[block] = jnp.where(low, a, pltpu.roll(b, 64, 1)).astype(BF16)
                 prod_send[block + 1] = jnp.where(low, pltpu.roll(a, 64, 1), b).astype(BF16)
-    products = (prod_send, prod_in, ps, pr, pl_)
-    all_to_all_start(*products)
+        if slab == 0:
+            pltpu.make_async_copy(prod_send.at[dev], prod_in.at[dev], pl_).start()
+        send_product(slab, 1 if slab == 0 else 0)
 
     own_sent = grid_col == col
 
@@ -611,7 +720,8 @@
             pltpu.VMEM((2048, 128), F32),
             pltpu.VMEM((2048, 128), F32),
         ]
-        + [pltpu.SemaphoreType.DMA] * 9,
+        + [pltpu.SemaphoreType.DMA] * 9
+        + EVERYONE,
         compiler_params=pltpu.CompilerParams(
             collective_id=2, has_side_effects=True, vmem_limit_bytes=VMEM_LIMIT
         ),
@@ -637,11 +747,11 @@
 ):
     ids = chain_ids.reshape(1, 512)
     row_w, col_w = row_bias_proj.T, col_bias_proj.T
-    g_rows, *projected = start(pair_rep, row_w, row_project)
-    mix = attention(0, tile_mask, chain_bias, g_rows, ids, row_w, projected)
-    g_cols, *projected, cols = middle(pair_rep, mix, row_output, col_w, col_project)
-    mix = attention(1, tile_mask, chain_bias, g_cols, ids, col_w, projected)
-    return triangle(tile_mask, cols, mix, col_output, tri_left, tri_right, tri_gate, tri_output)
+    g, *projected, steps, mask, add, ids = start(pair_rep, row_w, row_project, tile_mask, chain_bias, ids)
+    mix = attention(0, mask, add, g, ids, steps, projected)
+    g, *projected, steps, cols = middle(pair_rep, mix, row_output, col_w, col_project)
+    mix = attention(1, mask, add, g, ids, steps, projected)
+    return triangle(mask, cols, mix, col_output, tri_left, tri_right, tri_gate, tri_output)
 
 
 def solution(mesh):

time: 125 us -> 118 us (0.944)
  Pallas kernels: 118 us -> 112 us
    pallas_call x1, Pallas kernels: 49.8 us -> 45.5 us  [triangle(): pl.pallas_call(triangle_kernel, out_shape=jax.ShapeDtypeStruct((32, 64, 1...]
    pallas_call x1, Pallas kernels: 31.1 us -> 29.8 us  [middle(): pl.pallas_call(middle_kernel, out_shape=(jax.ShapeDtypeStruct(G_SHAPE, jn...]
    unnamed x35 -> x31, local copies, waits for them, and re-layouts: 6.71 us -> 5.52 us
where the time goes in v3:
time: 118 us; the launch traced here: 117 us
  Pallas kernels  112 us (95%)
  local copies, waits for them, and re-layouts  5.52 us (5%)
    pallas_call x1, Pallas kernels, triangle(): pl.pallas_call(triangle_kernel, out_shape=jax.ShapeDtypeStruct((32, 64, 1...  45.5 us
    pallas_call x1, Pallas kernels, middle(): pl.pallas_call(middle_kernel, out_shape=(jax.ShapeDtypeStruct(G_SHAPE, jn...  29.8 us
    pallas_call x1, Pallas kernels, start(): pl.pallas_call(start_kernel, out_shape=(jax.ShapeDtypeStruct(G_SHAPE, jnp...  25.5 us
    pallas_call x2, Pallas kernels, attention(): pl.pallas_call(functools.partial(attention_kernel, which), out_shape=jax....  10.9 us
    unnamed x31, local copies, waits for them, and re-layouts  5.52 us

profile of v3, /device:TPU:1, one launch (start us, length us, event | category | flops | bytes accessed | tf_op | source)
XLA Modules:
  0.0 117.4 jit_solution(17068861125948918286)
XLA Ops:
  0.0 0.0 copy-start
  0.0 1.0 copy-done
  1.0 0.0 copy-start.2
  1.0 0.9 copy-done.2
  1.9 0.0 copy-start.10
  1.9 0.7 copy-done.10
  2.6 0.0 copy-start.11
  2.6 0.7 copy-done.11
  3.3 0.0 copy-start.12
  3.3 0.7 copy-done.12
  4.0 0.0 copy-start.13
  4.0 0.7 copy-done.13
  4.7 25.5 %bias_gather.1 = (s16[2,128,2,16,128]{4,3,2,1,0:T(8,128)(2,1)S(1)}, bf16[4,512,128]{2,1,0:T(8,128)(2,1)S(1)}, bf16[4,128,512]{2,1,0:T(8,128)(2,1)S(1)}, bf16[4,1...) custom-call(bf16[4,512,128]{2,1,0:T(8,128)(2,1)S(1)} %copy-done, ...), custom_call_target="tpu_custom_call" | custom-call | tf_op jit(solution)/shard_map/bias_gather/pallas_call | solution.py:299
  30.2 0.0 copy-start.1
  30.2 0.0 copy-start.3
  30.2 0.0 copy-start.9
  30.2 0.0 copy-start.14
  30.2 6.2 %row_attention.1.mix_ref = bf16[4,128,512]{2,1,0:T(8,128)(2,1)S(1)} custom-call(s32[4,4]{1,0:T(4,128)S(1)} %get-tuple-element.21.mask_ref, f32[2,4]{1,0:T(2,128)S(1)} %get-tuple-element.22.add_ref, s16[2,128,2,16,128]{4,3,2,1,0:T(8,128)(2,1)S(1)} %get-tuple-element.23.g_ref, s32[1,512]{1,0:T(1,128)S(1)} %get-tuple-element.24.ids_ref, ...), custom_call_target="tpu_custom_call" | custom-call | tf_op jit(solution)/shard_map/row_attention/pallas_call | solution.py:530
  36.4 0.0 copy-done.1
  36.4 0.0 copy-done.3
  36.5 0.0 copy-done.9
  36.5 0.0 copy-done.14
  36.5 29.8 %columns_and_bias.1 = (s16[2,128,2,16,128]{4,3,2,1,0:T(8,128)(2,1)S(1)}, bf16[4,512,128]{2,1,0:T(8,128)(2,1)S(1)}, bf16[4,128,512]{2,1,0:T(8,128)(2,1)S(1)}, bf1...) custom-call(bf16[4,512,128]{2,1,0:T(8,128)(2,1)S(1)} %copy-done.1, ...), custom_call_target="tpu_custom_call" | custom-call | tf_op jit(solution)/shard_map/columns_and_bias/pallas_call | solution.py:415
  66.3 0.0 copy-start.4
  66.3 0.0 copy-start.5
  66.3 0.0 copy-start.6
  66.3 0.0 copy-start.7
  66.3 0.0 copy-start.8
  66.3 4.7 %col_attention.1.mix_ref = bf16[4,128,512]{2,1,0:T(8,128)(2,1)S(1)} custom-call(s32[4,4]{1,0:T(4,128)S(1)} %get-tuple-element.21.mask_ref, f32[2,4]{1,0:T(2,128)S(1)} %get-tuple-element.22.add_ref, s16[2,128,2,16,128]{4,3,2,1,0:T(8,128)(2,1)S(1)} %get-tuple-element.31.g_ref, s32[1,512]{1,0:T(1,128)S(1)} %get-tuple-element.24.ids_ref, ...), custom_call_target="tpu_custom_call" | custom-call | tf_op jit(solution)/shard_map/col_attention/pallas_call | solution.py:530
  71.0 0.0 copy-done.4
  71.0 0.0 copy-done.5
  71.1 0.0 copy-done.6
  71.1 0.0 copy-done.7
  71.1 0.0 copy-done.8
  71.1 45.5 %triangle.1 = bf16[32,64,128]{2,1,0:T(8,128)(2,1)S(1)} custom-call(s32[4,4]{1,0:T(4,128)S(1)} %get-tuple-element.21.mask_ref, bf16[128,16,128]{2,1,0:T(8,128)(2,1)S(1)} %get-tuple-element.30.cols_ref, bf16[4,128,512]{2,1,0:T(8,128)(2,1)S(1)} %col_attention.1.mix_ref, bf16[128,128]{1,0:T(8,128)(2,1)S(1)} %copy-done.6, bf16[128,256]{1,0:T(8,128)(2,1)S(1)} %copy-done.4, ...), custom_call_target="tpu_custom_call" | custom-call | tf_op jit(solution)/shard_map/triangle/pallas_call | solution.py:705
  116.6 0.8 copy.16
Async XLA Ops:
  0.0 1.0 copy-start
  1.0 0.9 copy-start.2
  1.9 0.7 copy-start.10
  2.6 0.7 copy-start.11
  3.3 0.7 copy-start.12
  4.0 0.7 copy-start.13
  30.2 6.3 %copy-start.1 = (bf16[4,512,128]{2,1,0:T(8,128)(2,1)S(1)}, bf16[4,512,128]{2,1,0:T(8,128)(2,1)}, u32[]{:S(2)}) copy-start(bf16[4,512,128]{2,1,0:T(8,128)(2,1)} %x_ref.1) | copy-start | bytes 1572868
  30.2 6.3 %copy-start.3 = (bf16[128,512]{1,0:T(8,128)(2,1)S(1)}, bf16[128,512]{1,0:T(8,128)(2,1)}, u32[]{:S(2)}) copy-start(bf16[128,512]{1,0:T(8,128)(2,1)} %project_ref.1) | copy-start | bytes 393220
  30.2 6.3 %copy-start.9 = (bf16[128,128]{1,0:T(8,128)(2,1)S(1)}, bf16[128,128]{1,0:T(8,128)(2,1)}, u32[]{:S(2)}) copy-start(bf16[128,128]{1,0:T(8,128)(2,1)} %output_ref.2) | copy-start | bytes 98308
  30.2 6.3 %copy-start.14 = (bf16[128,4]{0,1:T(4,128)(2,1)S(1)}, bf16[128,4]{0,1:T(4,128)(2,1)}, u32[]{:S(2)}) copy-start(bf16[128,4]{0,1:T(4,128)(2,1)} %param.22) | copy-start | bytes 3076
  66.3 4.8 %copy-start.4 = (bf16[128,256]{1,0:T(8,128)(2,1)S(1)}, bf16[128,256]{1,0:T(8,128)(2,1)}, u32[]{:S(2)}) copy-start(bf16[128,256]{1,0:T(8,128)(2,1)} %left_ref.1) | copy-start | bytes 196612
  66.3 4.8 %copy-start.5 = (bf16[128,256]{1,0:T(8,128)(2,1)S(1)}, bf16[128,256]{1,0:T(8,128)(2,1)}, u32[]{:S(2)}) copy-start(bf16[128,256]{1,0:T(8,128)(2,1)} %right_ref.1) | copy-start | bytes 196612
  66.3 4.8 %copy-start.6 = (bf16[128,128]{1,0:T(8,128)(2,1)S(1)}, bf16[128,128]{1,0:T(8,128)(2,1)}, u32[]{:S(2)}) copy-start(bf16[128,128]{1,0:T(8,128)(2,1)} %output_ref.3) | copy-start | bytes 98308
  66.3 4.8 %copy-start.7 = (bf16[128,128]{1,0:T(8,128)(2,1)S(1)}, bf16[128,128]{1,0:T(8,128)(2,1)}, u32[]{:S(2)}) copy-start(bf16[128,128]{1,0:T(8,128)(2,1)} %gate_w_ref.1) | copy-start | bytes 98308
  66.3 4.7 %copy-start.8 = (bf16[128,128]{1,0:T(8,128)(2,1)S(1)}, bf16[128,128]{1,0:T(8,128)(2,1)}, u32[]{:S(2)}) copy-start(bf16[128,128]{1,0:T(8,128)(2,1)} %out_w_ref.1) | copy-start | bytes 98308

commit v4 on v3

--- a/solution.py
+++ b/solution.py
@@ -16,12 +16,12 @@
 VMEM_LIMIT = 24 * 2**20
 
 
+def cost(microseconds):
+    return pl.CostEstimate(flops=int(microseconds * 1.1e9), bytes_accessed=4 * 2**20, transcendentals=0)
+
+
 def vmem():
     return pl.BlockSpec(memory_space=pltpu.VMEM)
-
-
-def hbm():
-    return pl.BlockSpec(memory_space=pltpu.HBM)
 
 
 def smem():
@@ -119,25 +119,44 @@
 
 
 G_SHAPE = (2, 128, 2, 16, 128)
-GATHER_SEMS = [pltpu.SemaphoreType.DMA((n,)) for n in (1, 8, 8, 4, 4, 16, 16, 16, 16)]
-FORWARD = False
-
-
-def gather_bias(blk_ref, g_ref, own_sem, zs, zr, as_, ar_, bs, br, fs, fr, work=()):
+GATHER_SEMS = [pltpu.SemaphoreType.DMA] * 3 + [pltpu.SemaphoreType.DMA((16,))] * 4
+
+
+def near_row(half, offset):
+    row, _, _ = my_place()
+    y, x = row % 4, row // 4
+    return jnp.where(half == 0, x * 4 + lax.rem(y + offset, 4), lax.rem(x + offset, 4) * 4 + y)
+
+
+def far_row(half, offset):
+    return near_row(1 - half, offset)
+
+
+def signal_near():
+    row, col, _ = my_place()
+    core, z = col % 2, col // 2
+    barrier = pltpu.get_barrier_semaphore()
+
+    def step(i, carry):
+        place = lax.rem(z + i // 2 % 4, 4) * 2 + lax.rem(core + i, 2)
+        pl.semaphore_signal(barrier, inc=1, device_id=(near_row(core, i // 8), place), device_id_type=MESH)
+        return carry
+
+    lax.fori_loop(1, 32, step, 0)
+    for offset in (1, 2, 3):
+        pl.semaphore_signal(barrier, inc=1, device_id=(far_row(core, offset), col), device_id_type=MESH)
+    return 34
+
+
+def gather_bias(blk_ref, g_ref, own_sem, ns, nr, bs, br, fs, fr, work=()):
     row, col, dev = my_place()
     core, z, y, x = col % 2, col // 2, row % 4, row // 4
-    a_me = jnp.where(core == 0, y, x)
-    b_me = jnp.where(core == 0, x, y)
     sibling = (row, z * 2 + 1 - core)
     work = list(work)
 
     def do_work():
         if work:
             work.pop(0)()
-
-    def row_of(a, b):
-        a, b = lax.rem(a, 4), lax.rem(b, 4)
-        return jnp.where(core == 0, b * 4 + a, a * 4 + b)
 
     def part(half, start, size):
         return g_ref.at[half, pl.ds(start, size)]
@@ -151,74 +170,60 @@
         copy.start()
         started.append(copy)
 
-    near = [(1, 0), (3, 0), (0, 1), (1, 1), (3, 1), (2, 0), (2, 1)]
-    for step, flip in near:
-        to_core = lax.rem(core + flip, 2)
-        send(
-            blk_ref.at[pl.ds(to_core, 1)],
-            g_ref.at[pl.ds(to_core, 1), dev],
-            zs.at[step * 2 + flip],
-            zr.at[(4 - step) % 4 * 2 + flip],
-            (row, lax.rem(z + step, 4) * 2 + to_core),
-        )
-    own = pltpu.make_async_copy(blk_ref.at[pl.ds(core, 1)], g_ref.at[pl.ds(core, 1), dev], own_sem.at[0])
+    def send_near(half):
+        def step(i, carry):
+            to = lax.rem(i * 5, 16)
+            pltpu.make_async_remote_copy(
+                src_ref=blk_ref.at[pl.ds(half, 1)],
+                dst_ref=g_ref.at[pl.ds(half, 1), dev],
+                send_sem=ns,
+                recv_sem=nr,
+                device_id=(near_row(half, to // 4), lax.rem(z + to, 4) * 2 + half),
+                device_id_type=MESH,
+            ).start()
+            return carry
+
+        return step
+
+    lax.fori_loop(1, 16, send_near(core), 0)
+    lax.fori_loop(0, 16, send_near(1 - core), 0)
+    own = pltpu.make_async_copy(blk_ref.at[pl.ds(core, 1)], g_ref.at[pl.ds(core, 1), dev], own_sem)
     own.start()
     do_work()
     own.wait()
-    for step, flip in near:
-        source = row * 8 + lax.rem(z + step, 4) * 2 + lax.rem(core + flip, 2)
-        drain(g_ref.at[pl.ds(core, 1), source], zr.at[step * 2 + flip])
+    drain(g_ref.at[0, pl.ds(0, 31)], nr)
+
+    def row_of(da, db):
+        dx, dy = jnp.where(core == 0, db, da), jnp.where(core == 0, da, db)
+        return lax.rem(x + dx, 4) * 4 + lax.rem(y + dy, 4)
 
     def block(da, db):
-        return part(core, row_of(a_me + da, b_me + db) * 8, 8)
+        return part(core, row_of(da, db) * 8, 8)
 
     def to_sibling(da, db):
         ref = block(da, db)
         send(ref, ref, fs.at[da * 4 + db], fr.at[da * 4 + db], sibling)
 
-    def along_b(da, db, step):
-        ref = block(da, db)
-        rel = (db - step) % 4
-        send(ref, ref, bs.at[da * 4 + rel], br.at[da * 4 + rel], (row_of(a_me, b_me + step), col))
-
-    def spread(da):
-        along_b(da, 0, 1)
-        along_b(da, 0, 3)
-        if not FORWARD:
-            along_b(da, 0, 2)
+    for step in (1, 3, 2):
+        for da in range(4):
+            ref = block(da, 0)
+            rel = 4 - step
+            send(ref, ref, bs.at[da * 4 + rel], br.at[da * 4 + rel], (row_of(0, step), col))
+    for da in range(4):
         to_sibling(da, 0)
-
-    for step in (1, 3, 2):
-        ref = block(0, 0)
-        send(ref, ref, as_.at[step], ar_.at[4 - step], (row_of(a_me + step, b_me), col))
-    spread(0)
     do_work()
-    for da in (1, 3, 2):
-        drain(block(da, 0), ar_.at[da])
-        spread(da)
-    do_work()
-    for da in (0, 1, 3, 2):
-        for db in (3, 1):
+    for db in (3, 1, 2):
+        for da in range(4):
             drain(block(da, db), br.at[da * 4 + db])
-            if FORWARD and (db == 3) == (da in (0, 3)):
-                along_b(da, db, 1 if db == 3 else 3)
             to_sibling(da, db)
-    do_work()
-    for da in (0, 1, 3, 2):
-        drain(block(da, 2), br.at[da * 4 + 2])
-        to_sibling(da, 2)
     while work:
         do_work()
     for db in (0, 3, 1, 2):
-        for da in (0, 1, 3, 2):
-            s_row = jnp.where(
-                core == 1,
-                lax.rem(x + db, 4) * 4 + lax.rem(y + da, 4),
-                lax.rem(x + da, 4) * 4 + lax.rem(y + db, 4),
-            )
-            drain(part(1 - core, s_row * 8, 8), fr.at[da * 4 + db])
+        for da in range(4):
+            drain(part(1 - core, row_of(db, da) * 8, 8), fr.at[da * 4 + db])
     for copy in started:
         copy.wait_send()
+    drain(g_ref.at[0, pl.ds(0, 31)], ns)
 
 
 PROJECTED = (
@@ -241,82 +246,67 @@
 STEPS = jax.ShapeDtypeStruct((4, 128), F32)
 
 
+def first_kernel(out_ref):
+    out_ref[...] = jnp.zeros((8, 128), F32)
+
+
+def first():
+    return pl.pallas_call(
+        first_kernel,
+        out_shape=pltpu.VMEM((8, 128), F32),
+        out_specs=vmem(),
+        cost_estimate=cost(6),
+        name="first",
+    )()
+
+
 def start_kernel(
-    x_hbm,
-    bias_w_hbm,
-    project_hbm,
-    mask_hbm,
-    add_hbm,
-    ids_hbm,
+    first_ref,
+    x_ref,
+    bias_w_ref,
+    project_ref,
     g_ref,
     k_ref,
     q_ref,
     v_ref,
     gate_ref,
     steps_ref,
-    mask_ref,
-    add_ref,
-    ids_ref,
-    x_buf,
-    bias_w_buf,
-    project_buf,
     blk32,
     blk,
     normed_buf,
-    loaded,
     *sems,
 ):
-    loads = [pltpu.make_async_copy(bias_w_hbm, bias_w_buf, loaded.at[0])]
-    loads += [pltpu.make_async_copy(x_hbm.at[line], x_buf.at[line], loaded.at[1 + line]) for line in range(4)]
-    loads.append(pltpu.make_async_copy(project_hbm, project_buf, loaded.at[5]))
-    pairs = ((mask_hbm, mask_ref), (add_hbm, add_ref), (ids_hbm, ids_ref))
-    loads += [pltpu.make_async_copy(src, dst, loaded.at[6 + i]) for i, (src, dst) in enumerate(pairs)]
-    for load in loads:
-        load.start()
-    signals = signal_partners()
-    loads[0].wait()
-    step = bias_step(bias_w_buf)
+    signals = signal_near()
+    step = bias_step(bias_w_ref)
     steps_ref[...] = jnp.broadcast_to(step, (4, 128))
     inverse = 1.0 / step
     for line in range(4):
-        loads[1 + line].wait()
-        normed = layer_norm(x_buf[line].astype(F32)).astype(BF16)
+        normed = layer_norm(x_ref[line].astype(F32)).astype(BF16)
         normed_buf[line] = normed
-        code_bias(blk32, line, bias_w_buf, inverse, normed)
+        code_bias(blk32, line, bias_w_ref, inverse, normed)
     blk[...] = blk32[...].astype(jnp.int16)
     await_signals(signals)
 
-    def work(line):
-        if line == 0:
-            for load in loads[5:]:
-                load.wait()
-        project_line(line, normed_buf[line], project_buf, k_ref, q_ref, v_ref, gate_ref)
-
-    gather_bias(blk, g_ref, *sems, work=[functools.partial(work, line) for line in range(4)])
-
-
-def start(x, bias_w, project, mask, add, ids):
+    def work(lines):
+        for line in lines:
+            project_line(line, normed_buf[line], project_ref, k_ref, q_ref, v_ref, gate_ref)
+
+    gather_bias(blk, g_ref, *sems, work=[functools.partial(work, lines) for lines in ((0, 1), (2, 3))])
+
+
+def start(x, bias_w, project):
     return pl.pallas_call(
         start_kernel,
-        out_shape=(jax.ShapeDtypeStruct(G_SHAPE, jnp.int16),)
-        + PROJECTED
-        + (STEPS,)
-        + tuple(jax.ShapeDtypeStruct(a.shape, a.dtype) for a in (mask, add, ids)),
-        in_specs=[hbm()] * 6,
-        out_specs=(vmem(),) * 9,
-        scratch_shapes=[
-            pltpu.VMEM((4, 512, 128), BF16),
-            pltpu.VMEM((4, 128), BF16),
-            pltpu.VMEM((128, 512), BF16),
-        ]
-        + BLK
-        + [pltpu.VMEM((4, 512, 128), BF16), pltpu.SemaphoreType.DMA((9,))]
-        + GATHER_SEMS,
+        out_shape=(jax.ShapeDtypeStruct(G_SHAPE, jnp.int16),) + PROJECTED + (STEPS,),
+        in_specs=[vmem()] * 4,
+        out_specs=(vmem(),) * 6,
+        scratch_shapes=BLK + [pltpu.VMEM((4, 512, 128), BF16)] + GATHER_SEMS,
         compiler_params=pltpu.CompilerParams(
             collective_id=0, has_side_effects=True, vmem_limit_bytes=VMEM_LIMIT
         ),
+        cost_estimate=cost(20),
         name="bias_gather",
-    )(x, bias_w, project, mask, add, ids)
+    )(first(), x, bias_w, project)
 
 
 def all_to_all_some(src_ref, dst_ref, ssem, rsem, lsem, first, last):
@@ -406,7 +396,7 @@
             normed = layer_norm(cols_buf[pl.ds(line, 512, stride=4), :]).astype(BF16)
             project_line(line, normed, project_ref, k_ref, q_ref, v_ref, gate_ref)
 
-    work = [functools.partial(all_to_all_some, *args, lo, hi) for lo, hi in ((1, 33), (33, 81), (81, 128))]
+    work = [functools.partial(all_to_all_some, *args, lo, hi) for lo, hi in ((1, 65), (65, 128))]
     gather_bias(blk, g_ref, *sems, work=work + [project_all])
     all_to_all_sent(*args)
 
@@ -432,6 +422,7 @@
         compiler_params=pltpu.CompilerParams(
             collective_id=1, has_side_effects=True, vmem_limit_bytes=VMEM_LIMIT
         ),
+        cost_estimate=cost(28),
         name="columns_and_bias",
     )(x, mix, output, bias_w, project)
 
@@ -538,6 +529,7 @@
             pltpu.VMEM((4, 128, 128), F32),
         ],
         compiler_params=pltpu.CompilerParams(vmem_limit_bytes=VMEM_LIMIT),
+        cost_estimate=cost(6),
         name=("row_attention", "col_attention")[which],
     )(mask, add, g, ids, steps, *projected)
 
@@ -725,6 +717,7 @@
         compiler_params=pltpu.CompilerParams(
             collective_id=2, has_side_effects=True, vmem_limit_bytes=VMEM_LIMIT
         ),
+        cost_estimate=cost(38),
         name="triangle",
     )(mask, cols, mix, output, left, right, gate_w, out_w)
 
@@ -747,7 +740,8 @@
 ):
     ids = chain_ids.reshape(1, 512)
     row_w, col_w = row_bias_proj.T, col_bias_proj.T
-    g, *projected, steps, mask, add, ids = start(pair_rep, row_w, row_project, tile_mask, chain_bias, ids)
+    mask, add = tile_mask, chain_bias
+    g, *projected, steps = start(pair_rep, row_w, row_project)
     mix = attention(0, mask, add, g, ids, steps, projected)
     g, *projected, steps, cols = middle(pair_rep, mix, row_output, col_w, col_project)
     mix = attention(1, mask, add, g, ids, steps, projected)

time: 118 us -> 113 us (0.958)
  local copies, waits for them, and re-layouts: 5.52 us -> 1.91 us
    unnamed x31 -> x29, local copies, waits for them, and re-layouts: 5.52 us -> 1.91 us
    pallas_call x2, Pallas kernels: 10.9 us -> 9.34 us  [attention(): pl.pallas_call(functools.partial(attention_kernel, which), out_shape=jax....]
where the time goes in v4:
time: 113 us
  Pallas kernels  111 us (98%)
  local copies, waits for them, and re-layouts  1.91 us (2%)
    pallas_call x1, Pallas kernels, triangle(): pl.pallas_call(triangle_kernel, out_shape=jax.ShapeDtypeStruct((32, 64, 1...  46 us
    pallas_call x1, Pallas kernels, middle(): pl.pallas_call(middle_kernel, out_shape=(jax.ShapeDtypeStruct(G_SHAPE, jn...  29.8 us
    pallas_call x1, Pallas kernels, start(): pl.pallas_call(start_kernel, out_shape=(jax.ShapeDtypeStruct(G_SHAPE, jnp...  25.6 us
    pallas_call x2, Pallas kernels, attention(): pl.pallas_call(functools.partial(attention_kernel, which), out_shape=jax....  9.34 us

profile of v4, /device:TPU:1, one launch (start us, length us, event | category | flops | bytes accessed | tf_op | source)
XLA Modules:
  0.0 112.8 jit_solution(17966323600139491684)
XLA Ops:
  0.0 0.0 copy-start
  0.0 0.0 copy-start.1
  0.0 0.0 copy-start.11
  0.0 1.0 copy-done
  1.0 0.0 copy-done.1
  1.1 0.0 copy-done.11
  1.1 0.0 copy-start.9
  1.1 0.0 copy-start.10
  1.1 0.0 copy-start.13
  1.1 25.6 %bias_gather.1 = (s16[2,128,2,16,128]{4,3,2,1,0:T(8,128)(2,1)S(1)}, bf16[4,512,128]{2,1,0:T(8,128)(2,1)S(1)}, bf16[4,128,512]{2,1,0:T(8,128)(2,1)S(1)}, bf16[4,1...) custom-call(f32[8,128]{1,0:T(8,128)S(1)} %first.1.first_ref, ...), custom_call_target="tpu_custom_call" | custom-call | flops 22000001024 | bytes 4194304 | tf_op jit(solution)/shard_map/bias_gather/pallas_call | solution.py:298
  26.7 0.0 copy-done.9
  26.7 0.0 copy-done.10
  26.7 0.0 copy-done.13
  26.7 0.0 copy-start.2
  26.7 0.0 copy-start.5
  26.8 0.0 copy-start.12
  26.8 4.6 %row_attention.1.mix_ref = bf16[4,128,512]{2,1,0:T(8,128)(2,1)S(1)} custom-call(s32[4,4]{1,0:T(4,128)S(1)} %copy-done.10, f32[2,4]{1,0:T(2,128)S(1)} %copy-done.13, s16[2,128,2,16,128]{4,3,2,1,0:T(8,128)(2,1)S(1)} %get-tuple-element.18.g_ref, s32[1,512]{1,0:T(1,128)S(1)} %bitcast.3, f32[4,128]{1,0:T(4,128)S(1)} %get-tuple-element.19.steps_ref, ...), custom_call_target="tpu_custom_call" | custom-call | flops 6600000000 | bytes 4194304 | tf_op jit(solution)/shard_map/row_attention/pallas_call | solution.py:521
  31.4 0.0 copy-done.2
  31.4 0.0 copy-done.5
  31.4 0.0 copy-done.12
  31.4 29.8 %columns_and_bias.1 = (s16[2,128,2,16,128]{4,3,2,1,0:T(8,128)(2,1)S(1)}, bf16[4,512,128]{2,1,0:T(8,128)(2,1)S(1)}, bf16[4,128,512]{2,1,0:T(8,128)(2,1)S(1)}, bf1...) custom-call(bf16[4,512,128]{2,1,0:T(8,128)(2,1)S(1)} %copy-done, ...), custom_call_target="tpu_custom_call" | custom-call | flops 30799998976 | bytes 4194304 | tf_op jit(solution)/shard_map/columns_and_bias/pallas_call | solution.py:405
  61.2 0.0 copy-start.3
  61.2 0.0 copy-start.4
  61.3 0.0 copy-start.6
  61.3 0.0 copy-start.7
  61.3 0.0 copy-start.8
  61.3 4.7 %col_attention.1.mix_ref = bf16[4,128,512]{2,1,0:T(8,128)(2,1)S(1)} custom-call(s32[4,4]{1,0:T(4,128)S(1)} %copy-done.10, f32[2,4]{1,0:T(2,128)S(1)} %copy-done.13, s16[2,128,2,16,128]{4,3,2,1,0:T(8,128)(2,1)S(1)} %get-tuple-element.25.g_ref, s32[1,512]{1,0:T(1,128)S(1)} %bitcast.4, f32[4,128]{1,0:T(4,128)S(1)} %get-tuple-element.26.steps_ref, ...), custom_call_target="tpu_custom_call" | custom-call | flops 6600000000 | bytes 4194304 | tf_op jit(solution)/shard_map/col_attention/pallas_call | solution.py:521
  66.0 0.0 copy-done.3
  66.0 0.0 copy-done.4
  66.0 0.0 copy-done.6
  66.1 0.0 copy-done.7
  66.1 0.0 copy-done.8
  66.1 46.0 %triangle.1 = bf16[32,64,128]{2,1,0:T(8,128)(2,1)S(1)} custom-call(s32[4,4]{1,0:T(4,128)S(1)} %copy-done.10, bf16[128,16,128]{2,1,0:T(8,128)(2,1)S(1)} %get-tuple-element.24.cols_ref, bf16[4,128,512]{2,1,0:T(8,128)(2,1)S(1)} %col_attention.1.mix_ref, bf16[128,128]{1,0:T(8,128)(2,1)S(1)} %copy-done.6, bf16[128,256]{1,0:T(8,128)(2,1)S(1)} %copy-done.3, ...), custom_call_target="tpu_custom_call" | custom-call | flops 41799999488 | bytes 4194304 | tf_op jit(solution)/shard_map/triangle/pallas_call | solution.py:697
  112.0 0.8 copy.16
  (1 shorter events, 0.0 us)
Async XLA Ops:
  0.0 1.0 copy-start
  0.0 1.1 copy-start.1
  0.0 1.1 copy-start.11
  1.1 25.6 %copy-start.9 = (s32[512]{0:T(512)S(1)}, s32[512]{0:T(512)}, u32[]{:S(2)}) copy-start(s32[512]{0:T(512)} %param.16) | copy-start | bytes 6148
  1.1 25.6 %copy-start.10 = (s32[4,4]{1,0:T(4,128)S(1)}, s32[4,4]{1,0:T(4,128)}, u32[]{:S(2)}) copy-start(s32[4,4]{1,0:T(4,128)} %mask_ref.5) | copy-start | bytes 196
  1.1 25.6 %copy-start.13 = (f32[2,4]{1,0:T(2,128)S(1)}, f32[2,4]{1,0:T(2,128)}, u32[]{:S(2)}) copy-start(f32[2,4]{1,0:T(2,128)} %add_ref.3) | copy-start | bytes 100
  26.7 4.7 %copy-start.2 = (bf16[128,512]{1,0:T(8,128)(2,1)S(1)}, bf16[128,512]{1,0:T(8,128)(2,1)}, u32[]{:S(2)}) copy-start(bf16[128,512]{1,0:T(8,128)(2,1)} %project_ref.3) | copy-start | bytes 393220
  26.7 4.7 %copy-start.5 = (bf16[128,128]{1,0:T(8,128)(2,1)S(1)}, bf16[128,128]{1,0:T(8,128)(2,1)}, u32[]{:S(2)}) copy-start(bf16[128,128]{1,0:T(8,128)(2,1)} %output_ref.2) | copy-start | bytes 98308
  26.8 4.7 %copy-start.12 = (bf16[128,4]{0,1:T(4,128)(2,1)S(1)}, bf16[128,4]{0,1:T(4,128)(2,1)}, u32[]{:S(2)}) copy-start(bf16[128,4]{0,1:T(4,128)(2,1)} %param.22) | copy-start | bytes 3076
  61.2 4.8 %copy-start.3 = (bf16[128,256]{1,0:T(8,128)(2,1)S(1)}, bf16[128,256]{1,0:T(8,128)(2,1)}, u32[]{:S(2)}) copy-start(bf16[128,256]{1,0:T(8,128)(2,1)} %left_ref.1) | copy-start | bytes 196612
  61.2 4.8 %copy-start.4 = (bf16[128,256]{1,0:T(8,128)(2,1)S(1)}, bf16[128,256]{1,0:T(8,128)(2,1)}, u32[]{:S(2)}) copy-start(bf16[128,256]{1,0:T(8,128)(2,1)} %right_ref.1) | copy-start | bytes 196612
  61.3 4.8 %copy-start.6 = (bf16[128,128]{1,0:T(8,128)(2,1)S(1)}, bf16[128,128]{1,0:T(8,128)(2,1)}, u32[]{:S(2)}) copy-start(bf16[128,128]{1,0:T(8,128)(2,1)} %output_ref.3) | copy-start | bytes 98308
  61.3 4.8 %copy-start.7 = (bf16[128,128]{1,0:T(8,128)(2,1)S(1)}, bf16[128,128]{1,0:T(8,128)(2,1)}, u32[]{:S(2)}) copy-start(bf16[128,128]{1,0:T(8,128)(2,1)} %gate_w_ref.1) | copy-start | bytes 98308
  61.3 4.8 %copy-start.8 = (bf16[128,128]{1,0:T(8,128)(2,1)S(1)}, bf16[128,128]{1,0:T(8,128)(2,1)}, u32[]{:S(2)}) copy-start(bf16[128,128]{1,0:T(8,128)(2,1)} %out_w_ref.1) | copy-start | bytes 98308

commit v5 on v4

--- a/solution.py
+++ b/solution.py
@@ -71,47 +71,33 @@
         blk32[tile // 2, tile % 2, line * 4 : line * 4 + 4, :] = coded[:, tile * 128 : (tile + 1) * 128]
 
 
-def signal_partners():
-    row, col, _ = my_place()
-    core, z, y, x = col % 2, col // 2, row % 4, row // 4
-    partners = []
-    for step in range(4):
-        for flip in range(2):
-            if step or flip:
-                partners.append((row, lax.rem(z + step, 4) * 2 + lax.rem(core + flip, 2)))
-    for step in (1, 2, 3):
-        partners.append((x * 4 + lax.rem(y + step, 4), col))
-        partners.append((lax.rem(x + step, 4) * 4 + y, col))
-    barrier = pltpu.get_barrier_semaphore()
-    for partner in partners:
-        pl.semaphore_signal(barrier, inc=1, device_id=partner, device_id_type=MESH)
-    return len(partners)
-
-
 class Everyone:
-    def __init__(self, second, third):
-        self.second, self.third = second, third
-        self.count = signal_partners()
-
-    def next_round(self):
+    def __init__(self, second):
+        self.second = second
         row, col, _ = my_place()
         x, y = row // 4, row % 4
-        await_signals(self.count)
-        for step in (1, 2, 3):
-            for to in (x * 4 + lax.rem(y + step, 4), lax.rem(x + step, 4) * 4 + y):
-                pl.semaphore_signal(self.second, inc=1, device_id=(to, col), device_id_type=MESH)
-
-    def last_round(self):
-        row, col, _ = my_place()
-        pl.semaphore_wait(self.second, 6)
-        for step in range(1, 8):
-            pl.semaphore_signal(self.third, inc=1, device_id=(row, lax.rem(col + step, 8)), device_id_type=MESH)
+        barrier = pltpu.get_barrier_semaphore()
+
+        def step(i, carry):
+            to = (x * 4 + lax.rem(y + i // 8, 4), lax.rem(col + i, 8))
+            pl.semaphore_signal(barrier, inc=1, device_id=to, device_id_type=MESH)
+            return carry
+
+        lax.fori_loop(1, 32, step, 0)
+        self.line = [(lax.rem(x + offset, 4) * 4 + y, col) for offset in (1, 2, 3)]
+        for to in self.line:
+            pl.semaphore_signal(barrier, inc=1, device_id=to, device_id_type=MESH)
+
+    def next_round(self):
+        await_signals(34)
+        for to in self.line:
+            pl.semaphore_signal(self.second, inc=1, device_id=to, device_id_type=MESH)
 
     def wait(self):
-        pl.semaphore_wait(self.third, 7)
-
-
-EVERYONE = [pltpu.SemaphoreType.REGULAR] * 2
+        pl.semaphore_wait(self.second, 3)
+
+
+EVERYONE = [pltpu.SemaphoreType.REGULAR]
 
 
 def await_signals(count):
@@ -362,13 +348,12 @@
     blk32,
     blk,
     second_round,
-    third_round,
     s0,
     s1,
     s2,
     *sems,
 ):
-    everyone = Everyone(second_round, third_round)
+    everyone = Everyone(second_round)
     step = bias_step(bias_w_ref)
     steps_ref[...] = jnp.broadcast_to(step, (4, 128))
     inverse = 1.0 / step
@@ -380,10 +365,8 @@
         line_buf[line] = value
         for j in range(4):
             send_buf[pl.ds(line * 4 + j, 128, stride=16), :] = line_buf[line, pl.ds(j, 128, stride=4), :]
-        if line == 1:
+        if line == 2:
             everyone.next_round()
-        if line == 3:
-            everyone.last_round()
     blk[...] = blk32[...].astype(jnp.int16)
     tiles[...] = send_buf[...].reshape(128, 16, 128).astype(BF16)
     everyone.wait()
@@ -396,8 +379,7 @@
             normed = layer_norm(cols_buf[pl.ds(line, 512, stride=4), :]).astype(BF16)
             project_line(line, normed, project_ref, k_ref, q_ref, v_ref, gate_ref)
 
-    work = [functools.partial(all_to_all_some, *args, lo, hi) for lo, hi in ((1, 65), (65, 128))]
-    gather_bias(blk, g_ref, *sems, work=work + [project_all])
+    gather_bias(blk, g_ref, *sems, work=[functools.partial(all_to_all_start, *args), project_all])
     all_to_all_sent(*args)
 
 
@@ -565,10 +547,9 @@
     pr,
     pl_,
     second_round,
-    third_round,
 ):
     row, col, dev = my_place()
-    everyone = Everyone(second_round, third_round)
+    everyone = Everyone(second_round)
     flags = [mask_ref[tile, row // 4].astype(F32) for tile in range(4)]
     cols_buf[...] = cols_ref[...].astype(F32).reshape(2048, 128)
     w_o = output_ref[...]
@@ -584,10 +565,8 @@
                 edge_buf[pl.ds(line * 8 + side * 4 + tile, 128, stride=32), :] = (
                     act[:, tile * 128 : (tile + 1) * 128] * flags[tile]
                 )
-        if line == 1:
+        if line == 2:
             everyone.next_round()
-        if line == 3:
-            everyone.last_round()
     edge_ref[...] = edge_buf[...].reshape(128, 32, 128).astype(BF16)
     everyone.wait()
     edges = (edge_ref, edge_in, es, er, el)

time: 113 us -> 109 us (0.965)
  Pallas kernels: 111 us -> 107 us
    pallas_call x1, Pallas kernels: 46 us -> 43.4 us  [triangle(): pl.pallas_call(triangle_kernel, out_shape=jax.ShapeDtypeStruct((32, 64, 1...]
    pallas_call x1, Pallas kernels: 29.8 us -> 28.5 us  [middle(): pl.pallas_call(middle_kernel, out_shape=(jax.ShapeDtypeStruct(G_SHAPE, jn...]
where the time goes in v5:
time: 109 us
  Pallas kernels  107 us (98%)
  local copies, waits for them, and re-layouts  1.91 us (2%)
    pallas_call x1, Pallas kernels, triangle(): pl.pallas_call(triangle_kernel, out_shape=jax.ShapeDtypeStruct((32, 64, 1...  43.4 us
    pallas_call x1, Pallas kernels, middle(): pl.pallas_call(middle_kernel, out_shape=(jax.ShapeDtypeStruct(G_SHAPE, jn...  28.5 us
    pallas_call x1, Pallas kernels, start(): pl.pallas_call(start_kernel, out_shape=(jax.ShapeDtypeStruct(G_SHAPE, jnp...  25.6 us
    pallas_call x2, Pallas kernels, attention(): pl.pallas_call(functools.partial(attention_kernel, which), out_shape=jax....  9.33 us

profile of v5, /device:TPU:1, one launch (start us, length us, event | category | flops | bytes accessed | tf_op | source)
XLA Modules:
  0.0 108.9 jit_solution(12155501552911396128)
XLA Ops:
  0.0 0.0 copy-start
  0.0 0.0 copy-start.1
  0.0 0.0 copy-start.11
  0.0 1.0 copy-done
  1.0 0.0 copy-done.1
  1.1 0.0 copy-done.11
  1.1 0.0 copy-start.9
  1.1 0.0 copy-start.10
  1.1 0.0 copy-start.13
  1.1 25.6 %bias_gather.1 = (s16[2,128,2,16,128]{4,3,2,1,0:T(8,128)(2,1)S(1)}, bf16[4,512,128]{2,1,0:T(8,128)(2,1)S(1)}, bf16[4,128,512]{2,1,0:T(8,128)(2,1)S(1)}, bf16[4,1...) custom-call(f32[8,128]{1,0:T(8,128)S(1)} %first.1.first_ref, ...), custom_call_target="tpu_custom_call" | custom-call | flops 22000001024 | bytes 4194304 | tf_op jit(solution)/shard_map/bias_gather/pallas_call | solution.py:284
  26.7 0.0 copy-done.9
  26.7 0.0 copy-done.10
  26.7 0.0 copy-done.13
  26.7 0.0 copy-start.2
  26.7 0.0 copy-start.5
  26.8 0.0 copy-start.12
  26.8 4.6 %row_attention.1.mix_ref = bf16[4,128,512]{2,1,0:T(8,128)(2,1)S(1)} custom-call(s32[4,4]{1,0:T(4,128)S(1)} %copy-done.10, f32[2,4]{1,0:T(2,128)S(1)} %copy-done.13, s16[2,128,2,16,128]{4,3,2,1,0:T(8,128)(2,1)S(1)} %get-tuple-element.18.g_ref, s32[1,512]{1,0:T(1,128)S(1)} %bitcast.3, f32[4,128]{1,0:T(4,128)S(1)} %get-tuple-element.19.steps_ref, ...), custom_call_target="tpu_custom_call" | custom-call | flops 6600000000 | bytes 4194304 | tf_op jit(solution)/shard_map/row_attention/pallas_call | solution.py:503
  31.4 0.0 copy-done.2
  31.4 0.0 copy-done.5
  31.4 0.0 copy-done.12
  31.4 28.5 %columns_and_bias.1 = (s16[2,128,2,16,128]{4,3,2,1,0:T(8,128)(2,1)S(1)}, bf16[4,512,128]{2,1,0:T(8,128)(2,1)S(1)}, bf16[4,128,512]{2,1,0:T(8,128)(2,1)S(1)}, bf1...) custom-call(bf16[4,512,128]{2,1,0:T(8,128)(2,1)S(1)} %copy-done, ...), custom_call_target="tpu_custom_call" | custom-call | flops 30799998976 | bytes 4194304 | tf_op jit(solution)/shard_map/columns_and_bias/pallas_call | solution.py:387
  59.9 0.0 copy-start.3
  59.9 0.0 copy-start.4
  59.9 0.0 copy-start.6
  59.9 0.0 copy-start.7
  59.9 0.0 copy-start.8
  59.9 4.7 %col_attention.1.mix_ref = bf16[4,128,512]{2,1,0:T(8,128)(2,1)S(1)} custom-call(s32[4,4]{1,0:T(4,128)S(1)} %copy-done.10, f32[2,4]{1,0:T(2,128)S(1)} %copy-done.13, s16[2,128,2,16,128]{4,3,2,1,0:T(8,128)(2,1)S(1)} %get-tuple-element.25.g_ref, s32[1,512]{1,0:T(1,128)S(1)} %bitcast.4, f32[4,128]{1,0:T(4,128)S(1)} %get-tuple-element.26.steps_ref, ...), custom_call_target="tpu_custom_call" | custom-call | flops 6600000000 | bytes 4194304 | tf_op jit(solution)/shard_map/col_attention/pallas_call | solution.py:503
  64.7 0.0 copy-done.3
  64.7 0.0 copy-done.4
  64.7 0.0 copy-done.6
  64.7 0.0 copy-done.7
  64.7 0.0 copy-done.8
  64.7 43.4 %triangle.1 = bf16[32,64,128]{2,1,0:T(8,128)(2,1)S(1)} custom-call(s32[4,4]{1,0:T(4,128)S(1)} %copy-done.10, bf16[128,16,128]{2,1,0:T(8,128)(2,1)S(1)} %get-tuple-element.24.cols_ref, bf16[4,128,512]{2,1,0:T(8,128)(2,1)S(1)} %col_attention.1.mix_ref, bf16[128,128]{1,0:T(8,128)(2,1)S(1)} %copy-done.6, bf16[128,256]{1,0:T(8,128)(2,1)S(1)} %copy-done.3, ...), custom_call_target="tpu_custom_call" | custom-call | flops 41799999488 | bytes 4194304 | tf_op jit(solution)/shard_map/triangle/pallas_call | solution.py:676
  108.1 0.8 copy.16
  (1 shorter events, 0.0 us)
Async XLA Ops:
  0.0 1.0 copy-start
  0.0 1.1 copy-start.1
  0.0 1.1 copy-start.11
  1.1 25.6 %copy-start.9 = (s32[512]{0:T(512)S(1)}, s32[512]{0:T(512)}, u32[]{:S(2)}) copy-start(s32[512]{0:T(512)} %param.16) | copy-start | bytes 6148
  1.1 25.6 %copy-start.10 = (s32[4,4]{1,0:T(4,128)S(1)}, s32[4,4]{1,0:T(4,128)}, u32[]{:S(2)}) copy-start(s32[4,4]{1,0:T(4,128)} %mask_ref.5) | copy-start | bytes 196
  1.1 25.6 %copy-start.13 = (f32[2,4]{1,0:T(2,128)S(1)}, f32[2,4]{1,0:T(2,128)}, u32[]{:S(2)}) copy-start(f32[2,4]{1,0:T(2,128)} %add_ref.3) | copy-start | bytes 100
  26.7 4.7 %copy-start.2 = (bf16[128,512]{1,0:T(8,128)(2,1)S(1)}, bf16[128,512]{1,0:T(8,128)(2,1)}, u32[]{:S(2)}) copy-start(bf16[128,512]{1,0:T(8,128)(2,1)} %project_ref.3) | copy-start | bytes 393220
  26.7 4.7 %copy-start.5 = (bf16[128,128]{1,0:T(8,128)(2,1)S(1)}, bf16[128,128]{1,0:T(8,128)(2,1)}, u32[]{:S(2)}) copy-start(bf16[128,128]{1,0:T(8,128)(2,1)} %output_ref.2) | copy-start | bytes 98308
  26.8 4.7 %copy-start.12 = (bf16[128,4]{0,1:T(4,128)(2,1)S(1)}, bf16[128,4]{0,1:T(4,128)(2,1)}, u32[]{:S(2)}) copy-start(bf16[128,4]{0,1:T(4,128)(2,1)} %param.22) | copy-start | bytes 3076
  59.9 4.8 %copy-start.3 = (bf16[128,256]{1,0:T(8,128)(2,1)S(1)}, bf16[128,256]{1,0:T(8,128)(2,1)}, u32[]{:S(2)}) copy-start(bf16[128,256]{1,0:T(8,128)(2,1)} %left_ref.1) | copy-start | bytes 196612
  59.9 4.8 %copy-start.4 = (bf16[128,256]{1,0:T(8,128)(2,1)S(1)}, bf16[128,256]{1,0:T(8,128)(2,1)}, u32[]{:S(2)}) copy-start(bf16[128,256]{1,0:T(8,128)(2,1)} %right_ref.1) | copy-start | bytes 196612
  59.9 4.8 %copy-start.6 = (bf16[128,128]{1,0:T(8,128)(2,1)S(1)}, bf16[128,128]{1,0:T(8,128)(2,1)}, u32[]{:S(2)}) copy-start(bf16[128,128]{1,0:T(8,128)(2,1)} %output_ref.3) | copy-start | bytes 98308
  59.9 4.8 %copy-start.7 = (bf16[128,128]{1,0:T(8,128)(2,1)S(1)}, bf16[128,128]{1,0:T(8,128)(2,1)}, u32[]{:S(2)}) copy-start(bf16[128,128]{1,0:T(8,128)(2,1)} %gate_w_ref.1) | copy-start | bytes 98308
  59.9 4.8 %copy-start.8 = (bf16[128,128]{1,0:T(8,128)(2,1)S(1)}, bf16[128,128]{1,0:T(8,128)(2,1)}, u32[]{:S(2)}) copy-start(bf16[128,128]{1,0:T(8,128)(2,1)} %out_w_ref.1) | copy-start | bytes 98308

commit v6 on v5

--- a/solution.py
+++ b/solution.py
@@ -493,7 +493,7 @@
                     mix_ref[line, at, q_at] = gated.astype(BF16)
             return carry
 
-        lax.fori_loop(0, 8, body, 0)
+        lax.fori_loop(0, 8, body, 0, unroll=(8, 4, 2, 2)[tiles - 1])
 
     for tiles in range(1, 5):
         pl.when(count == tiles)(functools.partial(run, tiles))

time: 109 us -> 106 us (0.972); the launches traced: 109 us -> 104 us
  Pallas kernels: 107 us -> 102 us
    pallas_call x2, Pallas kernels: 9.33 us -> 7.26 us  [attention(): pl.pallas_call(functools.partial(attention_kernel, which), out_shape=jax....]
    pallas_call x1, Pallas kernels: 28.5 us -> 26.8 us  [middle(): pl.pallas_call(middle_kernel, out_shape=(jax.ShapeDtypeStruct(G_SHAPE, jn...]
where the time goes in v6:
time: 106 us; the launch traced here: 104 us
  Pallas kernels  102 us (96%)
  local copies, waits for them, and re-layouts  1.91 us (2%)
    pallas_call x1, Pallas kernels, triangle(): pl.pallas_call(triangle_kernel, out_shape=jax.ShapeDtypeStruct((32, 64, 1...  42.5 us
    pallas_call x1, Pallas kernels, middle(): pl.pallas_call(middle_kernel, out_shape=(jax.ShapeDtypeStruct(G_SHAPE, jn...  26.8 us
    pallas_call x1, Pallas kernels, start(): pl.pallas_call(start_kernel, out_shape=(jax.ShapeDtypeStruct(G_SHAPE, jnp...  25.6 us
    pallas_call x2, Pallas kernels, attention(): pl.pallas_call(functools.partial(attention_kernel, which), out_shape=jax....  7.26 us

profile of v6, /device:TPU:1, one launch (start us, length us, event | category | flops | bytes accessed | tf_op | source)
XLA Modules:
  0.0 104.3 jit_solution(15161513769079126963)
XLA Ops:
  0.0 0.0 copy-start
  0.0 0.0 copy-start.1
  0.0 0.0 copy-start.11
  0.0 1.0 copy-done
  1.0 0.0 copy-done.1
  1.1 0.0 copy-done.11
  1.1 0.0 copy-start.9
  1.1 0.0 copy-start.10
  1.1 0.0 copy-start.13
  1.1 25.6 %bias_gather.1 = (s16[2,128,2,16,128]{4,3,2,1,0:T(8,128)(2,1)S(1)}, bf16[4,512,128]{2,1,0:T(8,128)(2,1)S(1)}, bf16[4,128,512]{2,1,0:T(8,128)(2,1)S(1)}, bf16[4,1...) custom-call(f32[8,128]{1,0:T(8,128)S(1)} %first.1.first_ref, ...), custom_call_target="tpu_custom_call" | custom-call | flops 22000001024 | bytes 4194304 | tf_op jit(solution)/shard_map/bias_gather/pallas_call | solution.py:284
  26.7 0.0 copy-done.9
  26.7 0.0 copy-done.10
  26.7 0.0 copy-done.13
  26.7 0.0 copy-start.2
  26.7 0.0 copy-start.5
  26.8 0.0 copy-start.12
  26.8 3.6 %row_attention.1.mix_ref = bf16[4,128,512]{2,1,0:T(8,128)(2,1)S(1)} custom-call(s32[4,4]{1,0:T(4,128)S(1)} %copy-done.10, f32[2,4]{1,0:T(2,128)S(1)} %copy-done.13, s16[2,128,2,16,128]{4,3,2,1,0:T(8,128)(2,1)S(1)} %get-tuple-element.18.g_ref, s32[1,512]{1,0:T(1,128)S(1)} %bitcast.3, f32[4,128]{1,0:T(4,128)S(1)} %get-tuple-element.19.steps_ref, ...), custom_call_target="tpu_custom_call" | custom-call | flops 6600000000 | bytes 4194304 | tf_op jit(solution)/shard_map/row_attention/pallas_call | solution.py:503
  30.4 0.0 copy-done.2
  30.4 0.0 copy-done.5
  30.4 0.0 copy-done.12
  30.4 26.8 %columns_and_bias.1 = (s16[2,128,2,16,128]{4,3,2,1,0:T(8,128)(2,1)S(1)}, bf16[4,512,128]{2,1,0:T(8,128)(2,1)S(1)}, bf16[4,128,512]{2,1,0:T(8,128)(2,1)S(1)}, bf1...) custom-call(bf16[4,512,128]{2,1,0:T(8,128)(2,1)S(1)} %copy-done, ...), custom_call_target="tpu_custom_call" | custom-call | flops 30799998976 | bytes 4194304 | tf_op jit(solution)/shard_map/columns_and_bias/pallas_call | solution.py:387
  57.2 0.0 copy-start.3
  57.2 0.0 copy-start.4
  57.2 0.0 copy-start.6
  57.3 0.0 copy-start.7
  57.3 0.0 copy-start.8
  57.3 3.7 %col_attention.1.mix_ref = bf16[4,128,512]{2,1,0:T(8,128)(2,1)S(1)} custom-call(s32[4,4]{1,0:T(4,128)S(1)} %copy-done.10, f32[2,4]{1,0:T(2,128)S(1)} %copy-done.13, s16[2,128,2,16,128]{4,3,2,1,0:T(8,128)(2,1)S(1)} %get-tuple-element.25.g_ref, s32[1,512]{1,0:T(1,128)S(1)} %bitcast.4, f32[4,128]{1,0:T(4,128)S(1)} %get-tuple-element.26.steps_ref, ...), custom_call_target="tpu_custom_call" | custom-call | flops 6600000000 | bytes 4194304 | tf_op jit(solution)/shard_map/col_attention/pallas_call | solution.py:503
  61.0 0.0 copy-done.3
  61.0 0.0 copy-done.4
  61.0 0.0 copy-done.6
  61.0 0.0 copy-done.7
  61.0 0.0 copy-done.8
  61.0 42.5 %triangle.1 = bf16[32,64,128]{2,1,0:T(8,128)(2,1)S(1)} custom-call(s32[4,4]{1,0:T(4,128)S(1)} %copy-done.10, bf16[128,16,128]{2,1,0:T(8,128)(2,1)S(1)} %get-tuple-element.24.cols_ref, bf16[4,128,512]{2,1,0:T(8,128)(2,1)S(1)} %col_attention.1.mix_ref, bf16[128,128]{1,0:T(8,128)(2,1)S(1)} %copy-done.6, bf16[128,256]{1,0:T(8,128)(2,1)S(1)} %copy-done.3, ...), custom_call_target="tpu_custom_call" | custom-call | flops 41799999488 | bytes 4194304 | tf_op jit(solution)/shard_map/triangle/pallas_call | solution.py:676
  103.5 0.8 copy.16
  (1 shorter events, 0.0 us)
Async XLA Ops:
  0.0 1.0 copy-start
  0.0 1.1 %copy-start.1 = (bf16[128,512]{1,0:T(8,128)(2,1)S(1)}, bf16[128,512]{1,0:T(8,128)(2,1)}, u32[]{:S(2)}) copy-start(bf16[128,512]{1,0:T(8,128)(2,1)} %project_ref.2) | copy-start | bytes 393220
  0.0 1.1 %copy-start.11 = (bf16[128,4]{0,1:T(4,128)(2,1)S(1)}, bf16[128,4]{0,1:T(4,128)(2,1)}, u32[]{:S(2)}) copy-start(bf16[128,4]{0,1:T(4,128)(2,1)} %param.19) | copy-start | bytes 3076
  1.1 25.6 %copy-start.9 = (s32[512]{0:T(512)S(1)}, s32[512]{0:T(512)}, u32[]{:S(2)}) copy-start(s32[512]{0:T(512)} %param.16) | copy-start | bytes 6148
  1.1 25.6 %copy-start.10 = (s32[4,4]{1,0:T(4,128)S(1)}, s32[4,4]{1,0:T(4,128)}, u32[]{:S(2)}) copy-start(s32[4,4]{1,0:T(4,128)} %mask_ref.5) | copy-start | bytes 196
  1.1 25.6 %copy-start.13 = (f32[2,4]{1,0:T(2,128)S(1)}, f32[2,4]{1,0:T(2,128)}, u32[]{:S(2)}) copy-start(f32[2,4]{1,0:T(2,128)} %add_ref.3) | copy-start | bytes 100
  26.7 3.6 %copy-start.2 = (bf16[128,512]{1,0:T(8,128)(2,1)S(1)}, bf16[128,512]{1,0:T(8,128)(2,1)}, u32[]{:S(2)}) copy-start(bf16[128,512]{1,0:T(8,128)(2,1)} %project_ref.3) | copy-start | bytes 393220
  26.7 3.6 %copy-start.5 = (bf16[128,128]{1,0:T(8,128)(2,1)S(1)}, bf16[128,128]{1,0:T(8,128)(2,1)}, u32[]{:S(2)}) copy-start(bf16[128,128]{1,0:T(8,128)(2,1)} %output_ref.2) | copy-start | bytes 98308
  26.8 3.6 %copy-start.12 = (bf16[128,4]{0,1:T(4,128)(2,1)S(1)}, bf16[128,4]{0,1:T(4,128)(2,1)}, u32[]{:S(2)}) copy-start(bf16[128,4]{0,1:T(4,128)(2,1)} %param.22) | copy-start | bytes 3076
  57.2 3.7 %copy-start.3 = (bf16[128,256]{1,0:T(8,128)(2,1)S(1)}, bf16[128,256]{1,0:T(8,128)(2,1)}, u32[]{:S(2)}) copy-start(bf16[128,256]{1,0:T(8,128)(2,1)} %left_ref.1) | copy-start | bytes 196612
  57.2 3.7 %copy-start.4 = (bf16[128,256]{1,0:T(8,128)(2,1)S(1)}, bf16[128,256]{1,0:T(8,128)(2,1)}, u32[]{:S(2)}) copy-start(bf16[128,256]{1,0:T(8,128)(2,1)} %right_ref.1) | copy-start | bytes 196612
  57.2 3.7 %copy-start.6 = (bf16[128,128]{1,0:T(8,128)(2,1)S(1)}, bf16[128,128]{1,0:T(8,128)(2,1)}, u32[]{:S(2)}) copy-start(bf16[128,128]{1,0:T(8,128)(2,1)} %output_ref.3) | copy-start | bytes 98308
  57.3 3.7 %copy-start.7 = (bf16[128,128]{1,0:T(8,128)(2,1)S(1)}, bf16[128,128]{1,0:T(8,128)(2,1)}, u32[]{:S(2)}) copy-start(bf16[128,128]{1,0:T(8,128)(2,1)} %gate_w_ref.1) | copy-start | bytes 98308
  57.3 3.7 %copy-start.8 = (bf16[128,128]{1,0:T(8,128)(2,1)S(1)}, bf16[128,128]{1,0:T(8,128)(2,1)}, u32[]{:S(2)}) copy-start(bf16[128,128]{1,0:T(8,128)(2,1)} %out_w_ref.1) | copy-start | bytes 98308

commit v7 on v6

--- a/solution.py
+++ b/solution.py
@@ -365,7 +365,7 @@
         line_buf[line] = value
         for j in range(4):
             send_buf[pl.ds(line * 4 + j, 128, stride=16), :] = line_buf[line, pl.ds(j, 128, stride=4), :]
-        if line == 2:
+        if line == 3:
             everyone.next_round()
     blk[...] = blk32[...].astype(jnp.int16)
     tiles[...] = send_buf[...].reshape(128, 16, 128).astype(BF16)
@@ -565,7 +565,7 @@
                 edge_buf[pl.ds(line * 8 + side * 4 + tile, 128, stride=32), :] = (
                     act[:, tile * 128 : (tile + 1) * 128] * flags[tile]
                 )
-        if line == 2:
+        if line == 3:
             everyone.next_round()
     edge_ref[...] = edge_buf[...].reshape(128, 32, 128).astype(BF16)
     everyone.wait()

time: 106 us -> 105 us (level); the launches traced: 104 us -> 105 us
    pallas_call x1, Pallas kernels: 42.5 us -> 44.7 us  [triangle(): pl.pallas_call(triangle_kernel, out_shape=jax.ShapeDtypeStruct((32, 64, 1...]
    pallas_call x1, Pallas kernels: 26.8 us -> 25.5 us  [middle(): pl.pallas_call(middle_kernel, out_shape=(jax.ShapeDtypeStruct(G_SHAPE, jn...]
where the time goes in v7:
time: 105 us
  Pallas kernels  103 us (98%)
  local copies, waits for them, and re-layouts  1.91 us (2%)
    pallas_call x1, Pallas kernels, triangle(): pl.pallas_call(triangle_kernel, out_shape=jax.ShapeDtypeStruct((32, 64, 1...  44.7 us
    pallas_call x1, Pallas kernels, start(): pl.pallas_call(start_kernel, out_shape=(jax.ShapeDtypeStruct(G_SHAPE, jnp...  25.6 us
    pallas_call x1, Pallas kernels, middle(): pl.pallas_call(middle_kernel, out_shape=(jax.ShapeDtypeStruct(G_SHAPE, jn...  25.5 us
    pallas_call x2, Pallas kernels, attention(): pl.pallas_call(functools.partial(attention_kernel, which), out_shape=jax....  7.26 us

profile of v7, /device:TPU:1, one launch (start us, length us, event | category | flops | bytes accessed | tf_op | source)
XLA Modules:
  0.0 105.2 jit_solution(12463178326710734187)
XLA Ops:
  0.0 0.0 copy-start
  0.0 0.0 copy-start.1
  0.0 0.0 copy-start.11
  0.0 1.0 copy-done
  1.0 0.0 copy-done.1
  1.1 0.0 copy-done.11
  1.1 0.0 copy-start.9
  1.1 0.0 copy-start.10
  1.1 0.0 copy-start.13
  1.1 25.6 %bias_gather.1 = (s16[2,128,2,16,128]{4,3,2,1,0:T(8,128)(2,1)S(1)}, bf16[4,512,128]{2,1,0:T(8,128)(2,1)S(1)}, bf16[4,128,512]{2,1,0:T(8,128)(2,1)S(1)}, bf16[4,1...) custom-call(f32[8,128]{1,0:T(8,128)S(1)} %first.1.first_ref, ...), custom_call_target="tpu_custom_call" | custom-call | flops 22000001024 | bytes 4194304 | tf_op jit(solution)/shard_map/bias_gather/pallas_call | solution.py:284
  26.7 0.0 copy-done.9
  26.7 0.0 copy-done.10
  26.7 0.0 copy-done.13
  26.7 0.0 copy-start.2
  26.7 0.0 copy-start.5
  26.8 0.0 copy-start.12
  26.8 3.6 %row_attention.1.mix_ref = bf16[4,128,512]{2,1,0:T(8,128)(2,1)S(1)} custom-call(s32[4,4]{1,0:T(4,128)S(1)} %copy-done.10, f32[2,4]{1,0:T(2,128)S(1)} %copy-done.13, s16[2,128,2,16,128]{4,3,2,1,0:T(8,128)(2,1)S(1)} %get-tuple-element.18.g_ref, s32[1,512]{1,0:T(1,128)S(1)} %bitcast.3, f32[4,128]{1,0:T(4,128)S(1)} %get-tuple-element.19.steps_ref, ...), custom_call_target="tpu_custom_call" | custom-call | flops 6600000000 | bytes 4194304 | tf_op jit(solution)/shard_map/row_attention/pallas_call | solution.py:503
  30.4 0.0 copy-done.2
  30.4 0.0 copy-done.5
  30.4 0.0 copy-done.12
  30.4 25.5 %columns_and_bias.1 = (s16[2,128,2,16,128]{4,3,2,1,0:T(8,128)(2,1)S(1)}, bf16[4,512,128]{2,1,0:T(8,128)(2,1)S(1)}, bf16[4,128,512]{2,1,0:T(8,128)(2,1)S(1)}, bf1...) custom-call(bf16[4,512,128]{2,1,0:T(8,128)(2,1)S(1)} %copy-done, ...), custom_call_target="tpu_custom_call" | custom-call | flops 30799998976 | bytes 4194304 | tf_op jit(solution)/shard_map/columns_and_bias/pallas_call | solution.py:387
  55.9 0.0 copy-start.3
  55.9 0.0 copy-start.4
  55.9 0.0 copy-start.6
  55.9 0.0 copy-start.7
  55.9 0.0 copy-start.8
  55.9 3.7 %col_attention.1.mix_ref = bf16[4,128,512]{2,1,0:T(8,128)(2,1)S(1)} custom-call(s32[4,4]{1,0:T(4,128)S(1)} %copy-done.10, f32[2,4]{1,0:T(2,128)S(1)} %copy-done.13, s16[2,128,2,16,128]{4,3,2,1,0:T(8,128)(2,1)S(1)} %get-tuple-element.25.g_ref, s32[1,512]{1,0:T(1,128)S(1)} %bitcast.4, f32[4,128]{1,0:T(4,128)S(1)} %get-tuple-element.26.steps_ref, ...), custom_call_target="tpu_custom_call" | custom-call | flops 6600000000 | bytes 4194304 | tf_op jit(solution)/shard_map/col_attention/pallas_call | solution.py:503
  59.6 0.0 copy-done.3
  59.6 0.0 copy-done.4
  59.6 0.0 copy-done.6
  59.6 0.0 copy-done.7
  59.6 0.0 copy-done.8
  59.6 44.7 %triangle.1 = bf16[32,64,128]{2,1,0:T(8,128)(2,1)S(1)} custom-call(s32[4,4]{1,0:T(4,128)S(1)} %copy-done.10, bf16[128,16,128]{2,1,0:T(8,128)(2,1)S(1)} %get-tuple-element.24.cols_ref, bf16[4,128,512]{2,1,0:T(8,128)(2,1)S(1)} %col_attention.1.mix_ref, bf16[128,128]{1,0:T(8,128)(2,1)S(1)} %copy-done.6, bf16[128,256]{1,0:T(8,128)(2,1)S(1)} %copy-done.3, ...), custom_call_target="tpu_custom_call" | custom-call | flops 41799999488 | bytes 4194304 | tf_op jit(solution)/shard_map/triangle/pallas_call | solution.py:676
  104.4 0.8 copy.16
  (1 shorter events, 0.0 us)
Async XLA Ops:
  0.0 1.0 copy-start
  0.0 1.1 %copy-start.1 = (bf16[128,512]{1,0:T(8,128)(2,1)S(1)}, bf16[128,512]{1,0:T(8,128)(2,1)}, u32[]{:S(2)}) copy-start(bf16[128,512]{1,0:T(8,128)(2,1)} %project_ref.2) | copy-start | bytes 393220
  0.0 1.1 %copy-start.11 = (bf16[128,4]{0,1:T(4,128)(2,1)S(1)}, bf16[128,4]{0,1:T(4,128)(2,1)}, u32[]{:S(2)}) copy-start(bf16[128,4]{0,1:T(4,128)(2,1)} %param.19) | copy-start | bytes 3076
  1.1 25.6 %copy-start.9 = (s32[512]{0:T(512)S(1)}, s32[512]{0:T(512)}, u32[]{:S(2)}) copy-start(s32[512]{0:T(512)} %param.16) | copy-start | bytes 6148
  1.1 25.6 %copy-start.10 = (s32[4,4]{1,0:T(4,128)S(1)}, s32[4,4]{1,0:T(4,128)}, u32[]{:S(2)}) copy-start(s32[4,4]{1,0:T(4,128)} %mask_ref.5) | copy-start | bytes 196
  1.1 25.6 %copy-start.13 = (f32[2,4]{1,0:T(2,128)S(1)}, f32[2,4]{1,0:T(2,128)}, u32[]{:S(2)}) copy-start(f32[2,4]{1,0:T(2,128)} %add_ref.3) | copy-start | bytes 100
  26.7 3.6 %copy-start.2 = (bf16[128,512]{1,0:T(8,128)(2,1)S(1)}, bf16[128,512]{1,0:T(8,128)(2,1)}, u32[]{:S(2)}) copy-start(bf16[128,512]{1,0:T(8,128)(2,1)} %project_ref.3) | copy-start | bytes 393220
  26.7 3.6 %copy-start.5 = (bf16[128,128]{1,0:T(8,128)(2,1)S(1)}, bf16[128,128]{1,0:T(8,128)(2,1)}, u32[]{:S(2)}) copy-start(bf16[128,128]{1,0:T(8,128)(2,1)} %output_ref.2) | copy-start | bytes 98308
  26.8 3.6 %copy-start.12 = (bf16[128,4]{0,1:T(4,128)(2,1)S(1)}, bf16[128,4]{0,1:T(4,128)(2,1)}, u32[]{:S(2)}) copy-start(bf16[128,4]{0,1:T(4,128)(2,1)} %param.22) | copy-start | bytes 3076
  55.9 3.7 %copy-start.3 = (bf16[128,256]{1,0:T(8,128)(2,1)S(1)}, bf16[128,256]{1,0:T(8,128)(2,1)}, u32[]{:S(2)}) copy-start(bf16[128,256]{1,0:T(8,128)(2,1)} %left_ref.1) | copy-start | bytes 196612
  55.9 3.7 %copy-start.4 = (bf16[128,256]{1,0:T(8,128)(2,1)S(1)}, bf16[128,256]{1,0:T(8,128)(2,1)}, u32[]{:S(2)}) copy-start(bf16[128,256]{1,0:T(8,128)(2,1)} %right_ref.1) | copy-start | bytes 196612
  55.9 3.7 %copy-start.6 = (bf16[128,128]{1,0:T(8,128)(2,1)S(1)}, bf16[128,128]{1,0:T(8,128)(2,1)}, u32[]{:S(2)}) copy-start(bf16[128,128]{1,0:T(8,128)(2,1)} %output_ref.3) | copy-start | bytes 98308
  55.9 3.7 %copy-start.7 = (bf16[128,128]{1,0:T(8,128)(2,1)S(1)}, bf16[128,128]{1,0:T(8,128)(2,1)}, u32[]{:S(2)}) copy-start(bf16[128,128]{1,0:T(8,128)(2,1)} %gate_w_ref.1) | copy-start | bytes 98308
  55.9 3.7 %copy-start.8 = (bf16[128,128]{1,0:T(8,128)(2,1)S(1)}, bf16[128,128]{1,0:T(8,128)(2,1)}, u32[]{:S(2)}) copy-start(bf16[128,128]{1,0:T(8,128)(2,1)} %out_w_ref.1) | copy-start | bytes 98308
